TPU v7x, 256 devices: a whole 4x4x8 slice. The times are simulated.
256 devices in a mesh: lat: 64 (over z, x, y_lo), lon: 4 (over y_hi, core).
Axes of the slice: x: 4, y: 4 (y_hi: 2, y_lo: 2; y = y_hi * 2 + y_lo), z: 8, core: 2. Of those that a mesh axis runs over, the one named last changes fastest.
Arguments:
- tokens: bfloat16 [2, 384, 48, 512], P(None, 'lat', 'lon'), may hold values from -6 to 6
- land_sea: int32 [384, 48], P('lat', 'lon'), may hold values 0 or 1
- pole_band: int32 [384], P('lat'), may hold values 0 or 1
- land_embedding: bfloat16 [512], replicated, may hold values from -6 to 6
- pole_embedding: bfloat16 [512], replicated, may hold values from -6 to 6
- attend_first: bfloat16 [512, 1536], replicated, may hold values from -0.25 to 0.25
- output_first: bfloat16 [512, 512], replicated, may hold values from -0.5 to 0.5
- attend_second: bfloat16 [512, 1536], replicated, may hold values from -0.25 to 0.25
- output_second: bfloat16 [512, 512], replicated, may hold values from -0.5 to 0.5
- cotangent: bfloat16 [2, 384, 48, 512], P(None, 'lat', 'lon'), may hold values from -6 to 6
Outputs:
- layer_out: bfloat16 [2, 384, 48, 512], P(None, 'lat', 'lon')
- tokens_grad: bfloat16 [2, 384, 48, 512], P(None, 'lat', 'lon')
- grad_attend_first: float32 [512, 1536], P('lat')
- grad_output_first: float32 [512, 512], P('lat')
- grad_attend_second: float32 [512, 1536], P('lat')
- grad_output_second: float32 [512, 512], P('lat')
All inputs are finite; a program needn't handle non-finite values. No bound on the sum of `land_sea` or of `pole_band` on one device may be relied on, other than what follows from the above.
Results may differ from a plain program's by a relative error of at most 0.02.
Values may be sent and summed in bfloat16 or wider, within the bound.
A program may use at most 128 MiB of HBM per device.

v0:
```python
import math

import jax
import jax.numpy as jnp
from jax import lax
from jax.sharding import PartitionSpec as P

HEADS = 16
WLAT = 6
WLON = 12


EPS = 1e-05


def passed_along(block, axis, distance):
    devices = range(lax.axis_size(axis))
    route = [((i - distance) % len(devices), i) for i in devices]
    return lax.ppermute(block, axis, route)


def for_sending(array):

    def short(part):
        return part.astype(jnp.bfloat16) if part.dtype == jnp.float32 else part

    return jax.tree.map(short, array)


def contract_rows(left, right):
    return lax.dot_general(
        left, right, (((0,), (0,)), ((), ())), preferred_element_type=jnp.float32
    )


def contract_cols(left, right):
    return lax.dot_general(
        left, right, (((1,), (1,)), ((), ())), preferred_element_type=jnp.float32
    )


def to_windows(grid_field):
    levels, lat_rows, lon_cols, features = grid_field.shape
    blocks = grid_field.reshape(levels, lat_rows // WLAT, WLAT, lon_cols // WLON, WLON, features)
    blocks = blocks.transpose(1, 3, 0, 2, 4, 5)
    return blocks.reshape(lat_rows // WLAT * (lon_cols // WLON), levels * WLAT * WLON, features)


def from_windows(blocks, levels, lat_rows, lon_cols):
    features = blocks.shape[-1]
    grid = blocks.reshape(lat_rows // WLAT, lon_cols // WLON, levels, WLAT, WLON, features)
    return grid.transpose(2, 0, 3, 1, 4, 5).reshape(levels, lat_rows, lon_cols, features)


def attend_forward(inputs, allowed, attend_weight, output_weight):
    window_count, window_size, features = inputs.shape
    per_head = features // HEADS
    centre = jnp.mean(inputs, axis=-1, keepdims=True)
    centred = inputs - centre
    spread = lax.rsqrt(jnp.mean(centred * centred, axis=-1, keepdims=True) + EPS)
    normed = centred * spread
    hidden = normed.astype(jnp.bfloat16).reshape(window_count * window_size, features)
    packed = jnp.dot(hidden, attend_weight, preferred_element_type=jnp.float32).astype(jnp.bfloat16)
    packed = packed.reshape(window_count, window_size, 3, HEADS, per_head)
    query_part = packed[:, :, 0]
    key_part = packed[:, :, 1]
    value_part = packed[:, :, 2]
    scores = jnp.einsum(
        "bqhd,bkhd->bhqk", query_part, key_part, preferred_element_type=jnp.float32
    ) * (1.0 / math.sqrt(per_head))
    weights = jnp.exp(scores) * allowed[:, None, :, :]
    attention = weights / jnp.sum(weights, axis=-1, keepdims=True)
    attention_low = attention.astype(jnp.bfloat16)
    mixed_heads = jnp.einsum(
        "bhqk,bkhd->bqhd", attention_low, value_part, preferred_element_type=jnp.float32
    )
    mixed_heads = mixed_heads.astype(jnp.bfloat16).reshape(window_count * window_size, features)
    outputs = inputs + jnp.dot(
        mixed_heads, output_weight, preferred_element_type=jnp.float32
    ).reshape(window_count, window_size, features)
    return (
        outputs,
        (
            normed,
            spread,
            hidden,
            query_part,
            key_part,
            value_part,
            attention,
            attention_low,
            mixed_heads,
        ),
    )


def attend_backward(saved, grad_out, keep_mask, attend_weight, output_weight):
    (
        normed,
        spread,
        hidden,
        query_part,
        key_part,
        value_part,
        attention,
        attention_low,
        mixed_heads,
    ) = saved
    window_count, window_size, features = grad_out.shape
    per_head = query_part.shape[3]
    grad_low = grad_out.astype(jnp.bfloat16)
    keep_low = keep_mask.astype(jnp.bfloat16)
    flat_grad = grad_low.reshape(window_count * window_size, features)
    kept_grad = (grad_low * keep_low[:, None, None]).reshape(window_count * window_size, features)
    output_grad = contract_rows(mixed_heads, kept_grad)
    grad_mixed = contract_cols(flat_grad, output_weight).astype(jnp.bfloat16)
    grad_mixed = grad_mixed.reshape(window_count, window_size, HEADS, per_head)
    grad_attention = jnp.einsum(
        "bqhd,bkhd->bhqk", grad_mixed, value_part, preferred_element_type=jnp.float32
    )
    grad_value = jnp.einsum(
        "bhqk,bqhd->bkhd", attention_low, grad_mixed, preferred_element_type=jnp.float32
    ).astype(jnp.bfloat16)
    inner = jnp.sum(attention * grad_attention, axis=-1, keepdims=True)
    grad_scores = (attention * (grad_attention - inner) * (1.0 / math.sqrt(per_head))).astype(
        jnp.bfloat16
    )
    grad_query = jnp.einsum(
        "bhqk,bkhd->bqhd", grad_scores, key_part, preferred_element_type=jnp.float32
    ).astype(jnp.bfloat16)
    grad_key = jnp.einsum(
        "bhqk,bqhd->bkhd", grad_scores, query_part, preferred_element_type=jnp.float32
    ).astype(jnp.bfloat16)
    grad_packed = jnp.stack([grad_query, grad_key, grad_value], axis=2).reshape(
        window_count, window_size * 3 * features
    )
    kept_packed = (grad_packed * keep_low[:, None]).reshape(
        window_count * window_size, 3 * features
    )
    grad_packed = grad_packed.reshape(window_count * window_size, 3 * features)
    attend_grad = contract_rows(hidden, kept_packed)
    grad_hidden = contract_cols(grad_packed, attend_weight).reshape(
        window_count, window_size, features
    )
    grad_inputs = grad_out + spread * (
        grad_hidden
        - jnp.mean(grad_hidden, axis=-1, keepdims=True)
        - normed * jnp.mean(grad_hidden * normed, axis=-1, keepdims=True)
    )
    return (grad_inputs, attend_grad, output_grad)


def extend_owned(grid_field):
    half_lat = WLAT // 2
    half_lon = WLON // 2
    above = passed_along(grid_field[:, :half_lat], "lat", -1)
    taller = jnp.concatenate([grid_field[:, half_lat:], above], axis=1)
    beyond = passed_along(taller[:, :, :half_lon], "lon", -1)
    return jnp.concatenate([taller[:, :, half_lon:], beyond], axis=2)


def return_output(patch):
    lat_rows = patch.shape[1]
    lon_cols = patch.shape[2]
    half_lat = WLAT // 2
    half_lon = WLON // 2
    before = passed_along(patch[:, :, lon_cols - half_lon :], "lon", 1)
    placed = jnp.concatenate([before, patch[:, :, : lon_cols - half_lon]], axis=2)
    below = passed_along(placed[:, lat_rows - half_lat :], "lat", 1)
    return jnp.concatenate([below, placed[:, : lat_rows - half_lat]], axis=1)


def return_grad(patch):
    lat_rows = patch.shape[1]
    lon_cols = patch.shape[2]
    half_lat = WLAT // 2
    half_lon = WLON // 2
    before = passed_along(patch[:, :, lon_cols - half_lon :].astype(jnp.bfloat16), "lon", 1).astype(
        jnp.float32
    )
    placed = jnp.concatenate([before, patch[:, :, : lon_cols - half_lon]], axis=2)
    below = passed_along(for_sending(placed[:, lat_rows - half_lat :]), "lat", 1)
    return jnp.concatenate([below, placed[:, : lat_rows - half_lat]], axis=1)


def local(
    tokens,
    land_sea,
    pole_band,
    land_embedding,
    pole_embedding,
    attend_first,
    output_first,
    attend_second,
    output_second,
    cotangent,
):
    levels, lat_rows, lon_cols, features = tokens.shape
    half_lat = WLAT // 2
    marked = (
        tokens.astype(jnp.float32)
        + land_sea.astype(jnp.float32)[None, :, :, None] * land_embedding.astype(jnp.float32)
        + pole_band.astype(jnp.float32)[None, :, None, None] * pole_embedding.astype(jnp.float32)
    ).astype(jnp.bfloat16)
    first_in = to_windows(marked).astype(jnp.float32)
    all_allowed = jnp.ones((first_in.shape[0], 1, first_in.shape[1]), jnp.float32)
    all_owned = jnp.ones((first_in.shape[0],), jnp.float32)
    first_out, first_saved = attend_forward(first_in, all_allowed, attend_first, output_first)
    middle = from_windows(first_out, levels, lat_rows, lon_cols).astype(jnp.bfloat16)
    lat_index = lax.axis_index("lat")
    lat_count = lax.axis_size("lat")
    is_last = lat_index == lat_count - 1
    row_group = ((jnp.arange(lat_rows) >= lat_rows - half_lat) & is_last).astype(jnp.float32)
    group_field = jnp.broadcast_to(row_group[None, :, None, None], (levels, lat_rows, lon_cols, 1))
    groups = to_windows(group_field)[..., 0]
    allowed = (groups[:, :, None] == groups[:, None, :]).astype(jnp.float32)
    second_in = to_windows(extend_owned(middle)).astype(jnp.float32)
    second_out, second_saved = attend_forward(second_in, allowed, attend_second, output_second)
    patch_out = from_windows(second_out, levels, lat_rows, lon_cols).astype(jnp.bfloat16)
    layer_out = return_output(patch_out)
    wide_grad = to_windows(extend_owned(cotangent)).astype(jnp.float32)
    owned_windows = jnp.ones((second_in.shape[0],), jnp.float32)
    second_dx, attend_grad_two, output_grad_two = attend_backward(
        second_saved, wide_grad, owned_windows, attend_second, output_second
    )
    carried = return_grad(from_windows(second_dx, levels, lat_rows, lon_cols))
    first_dx, attend_grad_one, output_grad_one = attend_backward(
        first_saved, to_windows(carried), all_owned, attend_first, output_first
    )
    tokens_grad = from_windows(first_dx, levels, lat_rows, lon_cols).astype(jnp.bfloat16)
    pieces = (
        lax.psum_scatter(attend_grad_one, "lat", scatter_dimension=0, tiled=True),
        lax.psum_scatter(output_grad_one, "lat", scatter_dimension=0, tiled=True),
        lax.psum_scatter(attend_grad_two, "lat", scatter_dimension=0, tiled=True),
        lax.psum_scatter(output_grad_two, "lat", scatter_dimension=0, tiled=True),
    )
    results = (
        lax.psum(pieces[0].astype(jnp.bfloat16), "lon").astype(jnp.float32),
        lax.psum(pieces[1].astype(jnp.bfloat16), "lon").astype(jnp.float32),
        lax.psum(pieces[2].astype(jnp.bfloat16), "lon").astype(jnp.float32),
        lax.psum(pieces[3].astype(jnp.bfloat16), "lon").astype(jnp.float32),
    )
    return (layer_out, tokens_grad, results[0], results[1], results[2], results[3])


def solution(mesh):
    placed = (
        P(None, "lat", "lon", None),
        P("lat", "lon"),
        P("lat"),
        P(),
        P(),
        P(),
        P(),
        P(),
        P(),
        P(None, "lat", "lon", None),
    )
    return jax.shard_map(
        local,
        mesh=mesh,
        in_specs=placed,
        out_specs=(
            P(None, "lat", "lon", None),
            P(None, "lat", "lon", None),
            P("lat", None),
            P("lat", None),
            P("lat", None),
            P("lat", None),
        ),
        check_vma=False,
    )
```

profile of v0, /device:TPU:1, one launch (start us, length us, event | category | flops | bytes accessed | tf_op | source)
XLA Modules:
  0.0 1391.7 jit_solution(5854556188323298482)
XLA Ops:
  7.2 1.8 fusion.120
  9.0 9.6 collective-permute-start.4
  21.5 1.8 fusion.116
  25.2 1.7 reshape.626
  26.9 1.4 broadcast_multiply_fusion.1
  37.3 2.4 collective-permute-done
  39.8 2.2 collective-permute-start.1
  43.9 2.8 collective-permute-done.1
  56.2 2.9 fusion.63
  62.6 6.0 fusion.43
  68.6 2.3 fusion.122
  71.1 6.0 fusion.40
  77.1 2.5 fusion.52
  81.5 1.8 reshape_transpose_reshape.7
  86.2 7.7 collective-permute-done.7
  95.5 2.3 fusion.121
  98.6 3.3 fusion.77
  104.8 2.1 convolution_convert_fusion.6
  108.0 1.9 fusion.61
  109.9 5.7 fusion.46
  115.6 5.7 fusion.49
  121.3 2.2 fusion.53
  123.8 2.4 fusion.74
  127.1 2.0 fusion.55
  130.1 5.4 collective-permute-start.2
  135.4 1.6 collective-permute-done.2
  137.2 2.2 fusion.112
  139.6 192.7 %reduce-scatter.11.cloned.1.call-done = f32[8,512]{1,0:T(8,128)} async-done(((f32[512,512]{1,0:T(8,128)}), f32[8,512]{1,0:T(8,128)}) %reduce-scatter.11.cloned.1.call-update) | async-done | bytes 16400 | tf_op jit(solution)/shard_map/reduce_scatter | solution.py:235
  333.7 311.5 %reduce-scatter.7.cloned.1.call-done = f32[8,512]{1,0:T(8,128)} async-done(((f32[512,512]{1,0:T(8,128)}), f32[8,512]{1,0:T(8,128)}) %reduce-scatter.7.cloned.1.call-update) | async-done | bytes 16400 | tf_op jit(solution)/shard_map/reduce_scatter | solution.py:233
  646.5 319.9 %reduce-scatter.9.cloned.1.call-done = f32[8,1536]{1,0:T(8,128)} async-done(((f32[512,1536]{1,0:T(8,128)}), f32[8,1536]{1,0:T(8,128)}) %reduce-scatter.9.cloned.1.call-update) | async-done | bytes 49168 | tf_op jit(solution)/shard_map/reduce_scatter | solution.py:234
  967.8 318.1 %reduce-scatter.5.cloned.1.call-done = f32[8,1536]{1,0:T(8,128)} async-done(((f32[512,1536]{1,0:T(8,128)}), f32[8,1536]{1,0:T(8,128)}) %reduce-scatter.5.cloned.1.call-update) | async-done | bytes 49168 | tf_op jit(solution)/shard_map/reduce_scatter | solution.py:232
  1289.1 90.8 %all-reduce.3.cloned.1.call-done = (bf16[8,1536]{1,0:T(8,128)(2,1)}, bf16[8,512]{1,0:T(8,128)(2,1)}, bf16[8,1536]{1,0:T(8,128)(2,1)}, bf16[8,512]{1,0:T(8,128)(2,1)}) async-done(((bf16[8,1536]{1,0:T(8,128)(2,1)}, bf16[8,512]{1,0:T(8,128)(2,1)}, bf16[8,1536]{1,0:T(8,128)(2,1)}, bf16[8,512]{1,0:T(8,128)(2,1)}), (bf16[8,1536]{1,0:T(8,128)(2,1)}, bf16[8,512]{1,0:T(8,128)(2,1)}, bf16[8,1536]{1,0:T(8,128)(2,1)}, ...) | async-done | bytes 65552 | tf_op jit(solution)/shard_map/psum | solution.py:238
  (139 shorter events, 54.6 us)
Async XLA Ops:
  7.2 46.5 %copy-start = (bf16[512,1536]{1,0:T(8,128)(2,1)S(1)}, bf16[512,1536]{1,0:T(8,128)(2,1)}, u32[]{:S(2)}) copy-start(bf16[512,1536]{1,0:T(8,128)(2,1)} %param.17) | copy-start | bytes 4718596
  7.2 23.3 %copy-start.1 = (bf16[512,1536]{1,0:T(8,128)(2,1)S(1)}, bf16[512,1536]{1,0:T(8,128)(2,1)}, u32[]{:S(2)}) copy-start(bf16[512,1536]{1,0:T(8,128)(2,1)} %param.15) | copy-start | bytes 4718596
  7.2 325.1 %reduce-scatter.11.cloned.1.call-start = ((), (), s32[]{:S(2)}) async-start(), calls=%async_computation.7 | async-start | bytes 1064960 | tf_op jit(solution)/shard_map/reduce_scatter | solution.py:235
  9.0 32.9 %collective-permute-start.4 = (bf16[2,3,12,512]{3,0,2,1:T(2,128)(2,1)}, bf16[2,3,12,512]{3,0,2,1:T(2,128)(2,1)}, u32[]{:S(2)}, u32[]{:S(2)}) collective-permute-start(bf16[2,3,12,512]{3,0,2,1:T(2,128)(2,1)} %get-tuple-element.57), channel_id=1, source_target_pairs={{4,0},{8,4},{12,8},{16,12},{20,16},{24,20},{28,24},{32,28},{36,32}... | collective-permute-start | bytes 221192 | tf_op jit(solution)/shard_map/ppermute | solution.py:19
  33.0 1.2 copy-start.3
  33.7 1.4 copy-start.7
  33.7 1.4 copy-start.20
  33.7 2.1 copy-start.10
  36.1 14.1 %copy-start.9 = (bf16[512,512]{1,0:T(8,128)(2,1)S(1)}, bf16[512,512]{1,0:T(8,128)(2,1)}, u32[]{:S(2)}) copy-start(bf16[512,512]{1,0:T(8,128)(2,1)} %param.18) | copy-start | bytes 1572868
  36.2 3.5 collective-permute-start
  39.8 7.0 collective-permute-start.1
  42.9 5.4 collective-permute-start.5
  56.2 2.9 copy-start.14
  59.9 1.4 copy-start.8
  70.9 574.3 %reduce-scatter.7.cloned.1.call-start = ((), (), s32[]{:S(2)}) async-start(), calls=%async_computation.5 | async-start | bytes 1064960 | tf_op jit(solution)/shard_map/reduce_scatter | solution.py:233
  77.1 2.5 copy-start.16
  77.1 2.5 copy-start.17
  84.3 1.7 collective-permute-start.6
  86.1 7.8 collective-permute-start.7
  97.8 868.6 %reduce-scatter.9.cloned.1.call-start = ((), (), s32[]{:S(2)}) async-start(), calls=%async_computation.6 | async-start | bytes 3194880 | tf_op jit(solution)/shard_map/reduce_scatter | solution.py:234
  102.0 1.0 copy-start.2
  102.0 6.0 copy-start.4
  102.0 1184.0 %reduce-scatter.5.cloned.1.call-start = ((), (), s32[]{:S(2)}) async-start(), calls=%async_computation.4 | async-start | bytes 3194880 | tf_op jit(solution)/shard_map/reduce_scatter | solution.py:232
  103.7 6.2 copy-start.21
  104.8 10.9 copy-start.5
  121.3 2.2 copy-start.18
  121.3 2.3 copy-start.19
  121.3 2.5 copy-start.11
  126.2 13.3 copy-start.6
  126.2 1253.7 %all-reduce.3.cloned.1.call-start = ((), (), s32[]{:S(2)}) async-start(), calls=%async_computation.8 | async-start | bytes 131072 | tf_op jit(solution)/shard_map/psum | solution.py:238
  130.1 7.0 collective-permute-start.2
  137.1 1150.3 %collective-permute-start.3 = (bf16[2,3,12,512]{3,2,1,0:T(8,128)(2,1)S(1)}, bf16[2,3,12,512]{3,2,1,0:T(8,128)(2,1)S(1)}, u32[]{:S(2)}, u32[]{:S(2)}) collective-permute-start(bf16[2,3,12,512]{3,2,1,0:T(8,128)(2,1)S(1)} %fusion.88), channel_id=1, source_target_pairs={{252,0},{0,4},{4,8},{8,12},{12,16},{16,20},{20,24},{24,28},{28,32}... | collective-permute-start | bytes 221192 | tf_op jit(solution)/shard_map/ppermute | solution.py:19
  (3 other events, 2.3 us)
Sparse Core Ops, SparseCore 0:
  71.0 261.2 reduce-scatter.10
  335.0 310.1 reduce-scatter.6
  647.7 318.6 reduce-scatter.8
  968.9 316.9 reduce-scatter.4
  1289.2 90.6 all-reduce.2
where the time goes:
time: 1390 us
  waiting for transfers between devices  1250 us (90%)
  matrix products  56.6 us (4%)
  local copies, waits for them, and re-layouts  28.7 us (2%)
  other arithmetic  24.7 us (2%)
  starting transfers between devices  19 us (1%)
  between operations  14.3 us (1%)
    reduce_scatter x1, waiting for transfers between devices, local(): lax.psum_scatter(attend_grad_two, 'lat', scatter_dimension=0, tiled=True)  320 us
    reduce_scatter x1, waiting for transfers between devices, local(): lax.psum_scatter(attend_grad_one, 'lat', scatter_dimension=0, tiled=True)  318 us
    reduce_scatter x1, waiting for transfers between devices, local(): lax.psum_scatter(output_grad_one, 'lat', scatter_dimension=0, tiled=True)  311 us
    reduce_scatter x1, waiting for transfers between devices, local(): lax.psum_scatter(output_grad_two, 'lat', scatter_dimension=0, tiled=True)  193 us
    psum x1, waiting for transfers between devices, local(): lax.psum(pieces[0].astype(jnp.bfloat16), 'lon').astype(jnp.float32)  90.8 us
  transfers between devices with their start and end apart: 13, of which 10 were waited for; matrix products, arithmetic and copies ran while one was open for 5% of the time, Pallas kernels for 0%

commit v1 on v0

v1 whole, which is shorter than its diff:
```python
import functools
import math

import jax
import jax.numpy as jnp
from jax import lax
from jax.experimental import pallas as pl
from jax.experimental.pallas import tpu as pltpu
from jax.sharding import PartitionSpec as P

MESH = pl.DeviceIdType.MESH
BF16 = jnp.bfloat16
F32 = jnp.float32

D = 512
HEADS = 16
PER_HEAD = D // HEADS
LV = 2
WLAT = 6
WLON = 12
CELLS = LV * WLAT * WLON
QUAD = CELLS // 4
SLAB = 48
EPS = 1e-05
SCALE = 1.0 / math.sqrt(PER_HEAD)
EXP2_SCALE = SCALE * math.log2(math.e)

NZ, NX, NYL = 8, 4, 2


def mm(left, right):
    return lax.dot_general(left, right, (((1,), (0,)), ((), ())), preferred_element_type=F32)


def mm_nt(left, right):
    return lax.dot_general(left, right, (((1,), (1,)), ((), ())), preferred_element_type=F32)


def quadrant(row, side):
    return (0 if row >= 3 else 1) + (0 if side == 1 else 2)


def chunk_offset(level, row, side):
    return quadrant(row, side) * QUAD + (level * 3 + row % 3) * 6


def slabs_to_cells(slab_ref, cells_ref):
    for level in range(LV):
        for row in range(WLAT):
            for side in range(2):
                off = chunk_offset(level, row, side)
                cells_ref[off : off + 6, :] = slab_ref[level * WLAT + row, side * 6 : side * 6 + 6, :]


def cells_to_field(cells_ref, slab_ref, field_ref):
    for level in range(LV):
        for row in range(WLAT):
            for side in range(2):
                off = chunk_offset(level, row, side)
                slab_ref[level * WLAT + row, side * 6 : side * 6 + 6, :] = cells_ref[off : off + 6, :]
            field_ref[level, row, :, :] = slab_ref[level * WLAT + row, 0:WLON, :].astype(BF16)


def layer_norm(u):
    centre = jnp.mean(u, axis=-1, keepdims=True)
    centred = u - centre
    spread = lax.rsqrt(jnp.mean(centred * centred, axis=-1, keepdims=True) + EPS)
    return centred * spread, spread


def head_lanes(head):
    lane = lax.broadcasted_iota(jnp.int32, (CELLS, 256), 1)
    return (lane // PER_HEAD) == (head % 8)


def forward(blk, w_ref, wo_ref, mask_ref):
    u = blk.u[...]
    normed, spread = layer_norm(u)
    blk.normed[...] = normed
    blk.spread[...] = jnp.broadcast_to(spread, (CELLS, 128))
    hidden = normed.astype(BF16)
    blk.hid_t[...] = hidden.T
    for part in range(3):
        cols = slice(part * D, part * D + D)
        packed = mm(hidden, w_ref[:, cols]).astype(BF16)
        blk.pk[:, cols] = packed
        blk.pk_t[cols, :] = packed.T

    def one_head(head):
        group = head // 8
        q_g = blk.pk[:, group * 256 : group * 256 + 256]
        k_g = blk.pk[:, D + group * 256 : D + group * 256 + 256]
        k_h = jnp.where(head_lanes(head), k_g, jnp.zeros_like(k_g))
        weights = jnp.exp2(mm_nt(k_h, q_g) * EXP2_SCALE)
        if mask_ref is not None:
            weights = weights * mask_ref[...]
        attention = (weights * (1.0 / jnp.sum(weights, axis=0, keepdims=True))).astype(BF16)
        blk.att[head] = attention
        rows = slice(head * PER_HEAD, head * PER_HEAD + PER_HEAD)
        v_t = blk.pk_t[2 * D + head * PER_HEAD : 2 * D + head * PER_HEAD + PER_HEAD, :]
        blk.mix_t[rows, :] = mm(v_t, attention)

    for head in range(HEADS):
        one_head(head)
    mixed = blk.mix_t[...].astype(BF16).T
    return u + mm(mixed, wo_ref[...])


def backward_heads(blk, wo_ref):
    dy_low = blk.dy[...].astype(BF16)
    blk.gm[...] = mm_nt(dy_low, wo_ref[...]).astype(BF16)
    blk.gm_t[...] = blk.gm[...].T

    def one_head(head):
        group = head // 8
        v_g = blk.pk[:, 2 * D + group * 256 : 2 * D + group * 256 + 256]
        g_g = blk.gm[:, group * 256 : group * 256 + 256]
        v_h = jnp.where(head_lanes(head), v_g, jnp.zeros_like(v_g))
        grad_attention = mm_nt(v_h, g_g)
        rows = slice(head * PER_HEAD, head * PER_HEAD + PER_HEAD)
        g_t = blk.gm_t[rows, :]
        inner = jnp.sum(blk.mix_t[rows, :] * g_t.astype(F32), axis=0, keepdims=True)
        attention = blk.att[head]
        grad_scores = (attention.astype(F32) * (grad_attention - inner)).astype(BF16)
        q_t = blk.pk_t[rows, :]
        k_t = blk.pk_t[D + head * PER_HEAD : D + head * PER_HEAD + PER_HEAD, :]
        blk.dpk_t[2 * D + head * PER_HEAD : 2 * D + head * PER_HEAD + PER_HEAD, :] = mm_nt(g_t, attention).astype(BF16)
        blk.dpk_t[rows, :] = (mm(k_t, grad_scores) * SCALE).astype(BF16)
        blk.dpk_t[D + head * PER_HEAD : D + head * PER_HEAD + PER_HEAD, :] = (mm_nt(q_t, grad_scores) * SCALE).astype(BF16)

    for head in range(HEADS):
        one_head(head)


def backward_input(blk, w_ref):
    grad_hidden = mm(w_ref[...], blk.dpk_t[...]).T
    normed = blk.normed[...]
    spread = blk.spread[:, 0:1]
    return blk.dy[...] + spread * (
        grad_hidden
        - jnp.mean(grad_hidden, axis=-1, keepdims=True)
        - normed * jnp.mean(grad_hidden * normed, axis=-1, keepdims=True)
    )


def pack_unit(first, second):
    first = first.reshape(64, 8, D)
    second = second.reshape(64, 8, D)
    return jnp.concatenate([first, second], axis=1).astype(BF16).reshape(NZ, NX, NYL, 16, D)


def output_and_value_unit(blk):
    grad_output = mm(blk.mix_t[...].astype(BF16), blk.dy[...].astype(BF16))
    grad_value = mm_nt(blk.hid_t[...], blk.dpk_t[2 * D :, :])
    return pack_unit(grad_output, grad_value)


def query_and_key_unit(blk):
    hid_t = blk.hid_t[...]
    return pack_unit(mm_nt(hid_t, blk.dpk_t[0:D, :]), mm_nt(hid_t, blk.dpk_t[D : 2 * D, :]))


BLOCK_SCRATCH = (
    ("u", (CELLS, D), F32),
    ("normed", (CELLS, D), F32),
    ("spread", (CELLS, 128), F32),
    ("hid_t", (D, CELLS), BF16),
    ("pk", (CELLS, 3 * D), BF16),
    ("pk_t", (3 * D, CELLS), BF16),
    ("att", (HEADS, CELLS, CELLS), BF16),
    ("mix_t", (D, CELLS), F32),
    ("dy", (CELLS, D), F32),
    ("gm", (CELLS, D), BF16),
    ("gm_t", (D, CELLS), BF16),
    ("dpk_t", (3 * D, CELLS), BF16),
)


class Block:
    def __init__(self, refs):
        for (name, _, _), ref in zip(BLOCK_SCRATCH, refs):
            setattr(self, name, ref)


class Torus:
    def __init__(self):
        self.lat = lax.axis_index("lat")
        self.lon = lax.axis_index("lon")
        self.z = self.lat // 8
        self.x = (self.lat // 2) % 4
        self.y = (self.lon // 2) * 2 + self.lat % 2
        self.core = self.lon % 2

    def at(self, x=None, y=None, z=None, core=None):
        x = self.x if x is None else x
        y = self.y if y is None else y
        z = self.z if z is None else z
        core = self.core if core is None else core
        return (z * 8 + x * 2 + y % 2, (y // 2) * 2 + core)

    def shifted(self, dlat, dlon):
        return ((self.lat + dlat + 64) % 64, (self.lon + dlon + 4) % 4)

    def greeted(self):
        found = [self.shifted(*step) for step in ((1, 0), (-1, 0), (1, 1), (-1, -1), (0, 1), (0, 2), (0, 3))]
        found += [self.at(y=(self.y + k) % 4) for k in (1, 3)]
        found += [self.at(x=(self.x + k) % 4) for k in (1, 2, 3)]
        found += [self.at(z=(self.z + k) % 8) for k in range(1, 8)]
        return found


class Halo:
    STEPS = ((1, 0), (0, 1), (1, 1))

    def __init__(self, torus, index, sign, out_ref, in_ref, send_sem, recv_sem):
        self.out_ref = out_ref.at[index]
        self.in_ref = in_ref.at[index]
        self.copies = [
            pltpu.make_async_remote_copy(
                src_ref=out_ref.at[index, n],
                dst_ref=in_ref.at[index, n],
                send_sem=send_sem.at[index, n],
                recv_sem=recv_sem.at[index, n],
                device_id=torus.shifted(sign * step[0], sign * step[1]),
                device_id_type=MESH,
            )
            for n, step in enumerate(self.STEPS)
        ]

    def send(self, cells_ref):
        for n, copy in enumerate(self.copies):
            q = n + 1
            self.out_ref[n, 0:QUAD, :] = cells_ref[q * QUAD : q * QUAD + QUAD, :].astype(BF16)
            copy.start()

    def receive(self, cells_ref):
        for n, copy in enumerate(self.copies):
            q = n + 1
            copy.wait_recv()
            cells_ref[q * QUAD : q * QUAD + QUAD, :] = self.in_ref[n, 0:QUAD, :].astype(F32)

    def close(self):
        for copy in self.copies:
            copy.wait_send()


REDUCE_SCRATCH = (
    ("whole", (4, NZ, NX, NYL, 16, D), BF16),
    ("core_in", (4, NZ, NX, NYL, 16, 256), BF16),
    ("s1", (4, NZ, NX, NYL, 16, 256), BF16),
    ("ya_in", (2, 3, NZ, NX, 16, 128), BF16),
    ("ya_sum", (2, NZ, NX, 16, 128), BF16),
    ("xa_in", (2, 3, NZ, 16, 128), BF16),
    ("xb_in", (2, 3, NZ, NYL, 16, 256), BF16),
    ("xb_sum", (2, NZ, NYL, 16, 256), BF16),
    ("yb_in", (2, 3, NZ, 16, 128), BF16),
    ("s3", (4, NZ, 16, 128), BF16),
    ("z_in", (4, 7, 16, 128), BF16),
    ("last", (4, 4, 16, 128), F32),
)
REDUCE_SEMS = 17


class Reduce:
    def __init__(self, torus, unit, bufs, send_sem, recv_sem):
        self.t, self.unit, self.b = torus, unit, bufs
        self.send_sem, self.recv_sem = send_sem.at[unit], recv_sem.at[unit]
        self.y_first = unit % 2 == 0
        self.half = unit // 2
        self.pending = []

    def _copy(self, src, dst, sem_out, sem_in, device):
        copy = pltpu.make_async_remote_copy(
            src_ref=src,
            dst_ref=dst,
            send_sem=self.send_sem.at[sem_out],
            recv_sem=self.recv_sem.at[sem_in],
            device_id=device,
            device_id_type=MESH,
        )
        copy.start()
        self.pending.append(copy)
        return copy

    def _axis(self, size, base, pick, landing, device):
        self.arriving = []
        for k in range(1, size):
            slot = size - k - 1
            self.arriving.append(self._copy(pick(k), landing.at[slot], base + slot, base + slot, device(k)))

    def _arrived(self):
        for copy in self.arriving:
            copy.wait_recv()

    def start(self):
        t, b, u = self.t, self.b, self.unit
        cols = pl.ds(pl.multiple_of((1 - t.core) * 256, 256), 256)
        self.arriving = [
            self._copy(b.whole.at[u, :, :, :, :, cols], b.core_in.at[u], 0, 0, t.at(core=1 - t.core))
        ]

    def _send_y(self, pick):
        t, b = self.t, self.b
        landing = b.ya_in.at[self.half] if self.y_first else b.yb_in.at[self.half]
        self._axis(4, 1, pick, landing, lambda k: t.at(y=(t.y + k) % 4))

    def _send_x(self, pick):
        t, b = self.t, self.b
        landing = b.xa_in.at[self.half] if self.y_first else b.xb_in.at[self.half]
        self._axis(4, 4, pick, landing, lambda k: t.at(x=(t.x + k) % 4))

    def _y_cols(self, k):
        return pl.ds(pl.multiple_of(((self.t.y + k) % 4) // 2 * 128, 128), 128)

    def after_core(self):
        t, b, u = self.t, self.b, self.unit
        self._arrived()
        cols = pl.ds(pl.multiple_of(t.core * 256, 256), 256)
        b.s1[u] = (b.whole[u, :, :, :, :, cols].astype(F32) + b.core_in[u].astype(F32)).astype(BF16)
        if self.y_first:
            self._send_y(lambda k: b.s1.at[u, :, :, (t.y + k) % 2, :, self._y_cols(k)])
        else:
            self._send_x(lambda k: b.s1.at[u, :, (t.x + k) % 4])

    def after_first(self):
        t, b, u, h = self.t, self.b, self.unit, self.half
        self._arrived()
        if self.y_first:
            total = b.s1[u, :, :, t.y % 2, :, self._y_cols(0)].astype(F32)
            for n in range(3):
                total = total + b.ya_in[h, n].astype(F32)
            b.ya_sum[h] = total.astype(BF16)
            self._send_x(lambda k: b.ya_sum.at[h, :, (t.x + k) % 4])
        else:
            total = b.s1[u, :, t.x].astype(F32)
            for n in range(3):
                total = total + b.xb_in[h, n].astype(F32)
            b.xb_sum[h] = total.astype(BF16)
            self._send_y(lambda k: b.xb_sum.at[h, :, (t.y + k) % 2, :, self._y_cols(k)])

    def after_second(self):
        t, b, u, h = self.t, self.b, self.unit, self.half
        self._arrived()
        if self.y_first:
            total, came = b.ya_sum[h, :, t.x].astype(F32), b.xa_in
        else:
            total, came = b.xb_sum[h, :, t.y % 2, :, self._y_cols(0)].astype(F32), b.yb_in
        for n in range(3):
            total = total + came[h, n].astype(F32)
        b.s3[u] = total.astype(BF16)
        self._axis(8, 7, lambda k: b.s3.at[u, (t.z + k) % 8], b.z_in.at[u], lambda k: t.at(z=(t.z + k) % 8))

    def after_z(self):
        t, b, u = self.t, self.b, self.unit
        self._arrived()
        total = b.s3[u, t.z].astype(F32)
        for n in range(7):
            total = total + b.z_in[u, n].astype(F32)
        b.last[u, t.lon] = total
        self.arriving = []
        for k in range(1, 4):
            slot = 4 - k - 1
            self.arriving.append(
                self._copy(b.last.at[u, t.lon], b.last.at[u, t.lon], 14 + slot, 14 + slot, t.shifted(0, k))
            )

    def finish(self, first_ref, first_col, second_ref, second_col):
        b, u = self.b, self.unit
        self._arrived()
        for lon in range(4):
            off = (lon % 2) * 256 + (lon // 2) * 128
            first_ref[:, first_col + off : first_col + off + 128] = b.last[u, lon, 0:8, :]
            second_ref[:, second_col + off : second_col + off + 128] = b.last[u, lon, 8:16, :]

    def close(self):
        for copy in self.pending:
            copy.wait_send()


class Named:
    pass


def kernel(
    tokens_ref,
    land_ref,
    pole_ref,
    land_vec_ref,
    pole_vec_ref,
    w1_hbm,
    o1_hbm,
    w2_hbm,
    o2_hbm,
    cot_ref,
    layer_ref,
    tokens_grad_ref,
    ga1_ref,
    go1_ref,
    ga2_ref,
    go2_ref,
    *scratch,
):
    n = len(BLOCK_SCRATCH)
    one, two = Block(scratch[:n]), Block(scratch[n : 2 * n])
    bufs = Named()
    for (name, _, _), ref in zip(REDUCE_SCRATCH, scratch[2 * n :]):
        setattr(bufs, name, ref)
    (w1_ref, o1_ref, w2_ref, o2_ref, slab_ref, cells_ref, mask_ref, halo_out, halo_in, load_sem, halo_send, halo_recv,
     red_send, red_recv) = scratch[2 * n + len(REDUCE_SCRATCH) :]

    torus = Torus()
    barrier = pltpu.get_barrier_semaphore()
    greeted = torus.greeted()
    for device in greeted:
        pl.semaphore_signal(barrier, inc=1, device_id=device, device_id_type=MESH)

    loads = [
        pltpu.make_async_copy(src, dst, load_sem.at[i])
        for i, (src, dst) in enumerate(((w1_hbm, w1_ref), (o1_hbm, o1_ref), (w2_hbm, w2_ref), (o2_hbm, o2_ref)))
    ]
    for load in loads:
        load.start()

    land = land_ref[...].astype(F32)
    eye = lax.broadcasted_iota(jnp.int32, (WLON, WLON), 0) == lax.broadcasted_iota(jnp.int32, (WLON, WLON), 1)
    land_vec = land_vec_ref[...].astype(F32)
    pole_vec = pole_vec_ref[...].astype(F32)
    for row in range(WLAT):
        marks = jnp.broadcast_to(land[row : row + 1, :], (WLON, WLON))
        column = jnp.sum(jnp.where(eye, marks, 0.0), axis=1, keepdims=True)
        on_land = column * land_vec
        polar = pole_ref[row].astype(F32) * pole_vec
        for level in range(LV):
            marked = tokens_ref[level, row, :, :].astype(F32) + on_land + polar
            slab_ref[level * WLAT + row, 0:WLON, :] = marked.astype(BF16).astype(F32)
    slabs_to_cells(slab_ref, one.u)

    for row in range(WLAT):
        for level in range(LV):
            slab_ref[level * WLAT + row, 0:WLON, :] = cot_ref[level, row, :, :].astype(F32)
    slabs_to_cells(slab_ref, two.dy)

    last = jnp.where(torus.lat == 63, 1.0, 0.0).astype(F32)
    far_k = (lax.broadcasted_iota(jnp.int32, (CELLS, CELLS), 0) // QUAD) % 2
    far_q = (lax.broadcasted_iota(jnp.int32, (CELLS, CELLS), 1) // QUAD) % 2
    mask_ref[...] = 1.0 - last * jnp.where(far_k == far_q, 0.0, 1.0)

    halos = [
        Halo(torus, i, sign, halo_out, halo_in, halo_send, halo_recv) for i, sign in enumerate((-1, -1, 1, 1))
    ]
    units = [Reduce(torus, u, bufs, red_send, red_recv) for u in range(4)]

    loads[0].wait()
    loads[1].wait()
    first = forward(one, w1_ref, o1_ref, None)
    two.u[...] = first.astype(BF16).astype(F32)

    pl.semaphore_wait(barrier, len(greeted))
    halos[0].send(two.u)
    halos[1].send(two.dy)
    loads[2].wait()
    loads[3].wait()
    halos[0].receive(two.u)
    cells_ref[...] = forward(two, w2_ref, o2_ref, mask_ref)
    halos[2].send(cells_ref)
    halos[1].receive(two.dy)

    backward_heads(two, o2_ref)
    one.dy[...] = backward_input(two, w2_ref)
    halos[3].send(one.dy)
    bufs.whole[0] = output_and_value_unit(two)
    units[0].start()
    bufs.whole[1] = query_and_key_unit(two)
    units[1].start()

    halos[3].receive(one.dy)
    units[0].after_core()
    backward_heads(one, o1_ref)
    units[1].after_core()
    bufs.whole[2] = output_and_value_unit(one)
    units[2].start()
    bufs.whole[3] = query_and_key_unit(one)
    units[3].start()
    units[0].after_first()
    units[1].after_first()

    halos[2].receive(cells_ref)
    cells_to_field(cells_ref, slab_ref, layer_ref)
    units[2].after_core()
    units[3].after_core()
    units[0].after_second()
    units[1].after_second()
    cells_ref[...] = backward_input(one, w1_ref)
    cells_to_field(cells_ref, slab_ref, tokens_grad_ref)
    units[2].after_first()
    units[3].after_first()
    units[0].after_z()
    units[1].after_z()
    units[2].after_second()
    units[3].after_second()
    units[0].finish(go2_ref, 0, ga2_ref, 2 * D)
    units[1].finish(ga2_ref, 0, ga2_ref, D)
    units[2].after_z()
    units[3].after_z()
    units[2].finish(go1_ref, 0, ga1_ref, 2 * D)
    units[3].finish(ga1_ref, 0, ga1_ref, D)
    for halo in halos:
        halo.close()
    for unit in units:
        unit.close()


def local(
    tokens,
    land_sea,
    pole_band,
    land_embedding,
    pole_embedding,
    attend_first,
    output_first,
    attend_second,
    output_second,
    cotangent,
):
    vmem = pl.BlockSpec(memory_space=pltpu.VMEM)
    smem = pl.BlockSpec(memory_space=pltpu.SMEM)
    hbm = pl.BlockSpec(memory_space=pl.ANY)
    field = jax.ShapeDtypeStruct(tokens.shape, BF16)
    return pl.pallas_call(
        kernel,
        out_shape=(
            field,
            field,
            jax.ShapeDtypeStruct((8, 3 * D), F32),
            jax.ShapeDtypeStruct((8, D), F32),
            jax.ShapeDtypeStruct((8, 3 * D), F32),
            jax.ShapeDtypeStruct((8, D), F32),
        ),
        in_specs=[vmem, vmem, smem, vmem, vmem, hbm, hbm, hbm, hbm, vmem],
        out_specs=[vmem] * 6,
        scratch_shapes=[pltpu.VMEM(shape, dtype) for _, shape, dtype in BLOCK_SCRATCH * 2 + REDUCE_SCRATCH]
        + [
            pltpu.VMEM((D, 3 * D), BF16),
            pltpu.VMEM((D, D), BF16),
            pltpu.VMEM((D, 3 * D), BF16),
            pltpu.VMEM((D, D), BF16),
            pltpu.VMEM((LV * WLAT, 16, D), F32),
            pltpu.VMEM((CELLS, D), F32),
            pltpu.VMEM((CELLS, CELLS), F32),
            pltpu.VMEM((4, 3, SLAB, D), BF16),
            pltpu.VMEM((4, 3, SLAB, D), BF16),
            pltpu.SemaphoreType.DMA((4,)),
            pltpu.SemaphoreType.DMA((4, 3)),
            pltpu.SemaphoreType.DMA((4, 3)),
            pltpu.SemaphoreType.DMA((4, REDUCE_SEMS)),
            pltpu.SemaphoreType.DMA((4, REDUCE_SEMS)),
        ],
        compiler_params=pltpu.CompilerParams(
            collective_id=0, has_side_effects=True, vmem_limit_bytes=56 * 1024 * 1024
        ),
    )(
        tokens,
        land_sea,
        pole_band,
        land_embedding.reshape(1, D),
        pole_embedding.reshape(1, D),
        attend_first,
        output_first,
        attend_second,
        output_second,
        cotangent,
    )


def solution(mesh):
    placed = (
        P(None, "lat", "lon", None),
        P("lat", "lon"),
        P("lat"),
        P(),
        P(),
        P(),
        P(),
        P(),
        P(),
        P(None, "lat", "lon", None),
    )
    return jax.shard_map(
        local,
        mesh=mesh,
        in_specs=placed,
        out_specs=(
            P(None, "lat", "lon", None),
            P(None, "lat", "lon", None),
            P("lat", None),
            P("lat", None),
            P("lat", None),
            P("lat", None),
        ),
        check_vma=False,
    )
```

time: 1390 us -> 83.1 us (0.06)
  waiting for transfers between devices: 1250 us -> 0 us
  Pallas kernels: 0 us -> 67.2 us
  matrix products: 56.6 us -> 0 us
  other arithmetic: 24.7 us -> 0 us
  starting transfers between devices: 19 us -> 0 us
  local copies, waits for them, and re-layouts: 28.7 us -> 14.7 us
    reduce_scatter x4 -> x0, waiting for transfers between devices: 1140 us -> none  [the longest x1 320 us: local(): lax.psum_scatter(attend_grad_two, 'lat', scatter_dimension=0, tiled=True)]
    psum x1 -> x0, waiting for transfers between devices: 90.8 us -> none  [local(): lax.psum(pieces[0].astype(jnp.bfloat16), 'lon').astype(jnp.float32)]
    pallas_call x0 -> x1, Pallas kernels: none -> 67.2 us  [local(): pl.pallas_call(kernel, out_shape=(field, field, jax.ShapeDtypeStruct((8,...]
    dot_general x24 -> x0, matrix products: 56.6 us -> none  [the longest x2 11.7 us: attend_backward(): jnp.einsum('bhqk,bqhd->bkhd', grad_scores, query_part, preferred_element_...]
    ppermute x8 -> x0, starting transfers between devices: 18.6 us -> none  [passed_along(): return lax.ppermute(block, axis, route)]
    convert_element_type x19 -> x0, other arithmetic: 15.4 us -> none  [the longest x1 1.41 us: local(): pieces[0].astype(jnp.bfloat16)]
    ppermute x8 -> x0, waiting for transfers between devices: 15.3 us -> none  [passed_along(): return lax.ppermute(block, axis, route)]
  transfers between devices with their start and end apart: 13 -> 0, of which waited for: 10 -> 0; matrix products, arithmetic and copies ran while one was open for 5% -> 0% of each run, Pallas kernels for 0% -> 0%
where the time goes in v1:
time: 83.1 us; the launch traced here: 82.6 us
  Pallas kernels  67.2 us (81%)
  local copies, waits for them, and re-layouts  14.7 us (18%)
    pallas_call x1, Pallas kernels, local(): pl.pallas_call(kernel, out_shape=(field, field, jax.ShapeDtypeStruct((8,...  67.2 us
    unnamed x6, local copies, waits for them, and re-layouts  8.71 us
    pallas_call x2, local copies, waits for them, and re-layouts, local(): pl.pallas_call(kernel, out_shape=(field, field, jax.ShapeDtypeStruct((8,...  3.48 us

profile of v1, /device:TPU:1, one launch (start us, length us, event | category | flops | bytes accessed | tf_op | source)
XLA Modules:
  0.0 82.6 jit_solution(15576112317072884626)
XLA Ops:
  0.6 1.3 %reshape.18.land_vec_ref = bf16[1,512]{1,0:T(2,128)(2,1)} reshape(bf16[512]{0:T(512)(128)(2,1)} %param.13) | data formatting | bytes 2048 | tf_op jit(solution)/shard_map/reshape | solution.py:565
  1.9 1.3 %reshape.19.pole_vec_ref = bf16[1,512]{1,0:T(2,128)(2,1)} reshape(bf16[512]{0:T(512)(128)(2,1)} %param.14) | data formatting | bytes 2048 | tf_op jit(solution)/shard_map/reshape | solution.py:566
  3.2 1.6 %copy.16.tokens_ref = bf16[2,6,12,512]{3,2,1,0:T(8,128)(2,1)} copy(bf16[2,6,12,512]{3,0,2,1:T(2,128)(2,1)} %param.10) | data formatting | bytes 294912 | tf_op args[0]
  4.8 1.6 %copy.17.cot_ref = bf16[2,6,12,512]{3,2,1,0:T(8,128)(2,1)} copy(bf16[2,6,12,512]{3,0,2,1:T(2,128)(2,1)} %param.19) | data formatting | bytes 294912 | tf_op args[9]
  6.4 67.2 %shard_map.145 = (bf16[2,6,12,512]{3,2,1,0:T(8,128)(2,1)}, bf16[2,6,12,512]{3,2,1,0:T(8,128)(2,1)}, f32[8,1536]{1,0:T(8,128)}, f32[8,512]{1,0:T(8,128)}, f32[8,1536]{1,0:T(8,128)}, /*index=5*/f32[8,512]{1,0:T(8,128)}) custom-call(bf16[2,6,12,512]{3,2,1,0:T(8,128)(2,1)} %copy.16.tokens_ref, s32[6,12]{1,0:T(8,128)} %land_ref.1, s32[6]{0:T(128)} %pole_ref.1, ...), custom_call_target="tpu_custom_call" | custom-call | tf_op jit(solution)/shard_map/pallas_call | solution.py:529
  73.6 1.7 %copy.18 = bf16[2,6,12,512]{3,0,2,1:T(2,128)(2,1)} copy(bf16[2,6,12,512]{3,2,1,0:T(8,128)(2,1)} %get-tuple-element.6) | data formatting | bytes 294912 | tf_op jit(solution)/shard_map/pallas_call | solution.py:529
  75.3 1.7 %copy.19 = bf16[2,6,12,512]{3,0,2,1:T(2,128)(2,1)} copy(bf16[2,6,12,512]{3,2,1,0:T(8,128)(2,1)} %get-tuple-element.7) | data formatting | bytes 294912 | tf_op jit(solution)/shard_map/pallas_call | solution.py:529
  77.1 1.4 %copy.24 = f32[8,1536]{1,0:T(8,128)} copy(f32[8,1536]{1,0:T(8,128)} %get-tuple-element.20) | data formatting | bytes 98304
  78.5 1.3 %copy.25 = f32[8,512]{1,0:T(8,128)} copy(f32[8,512]{1,0:T(8,128)} %get-tuple-element.21) | data formatting | bytes 32768
  79.8 1.4 %copy.26 = f32[8,1536]{1,0:T(8,128)} copy(f32[8,1536]{1,0:T(8,128)} %get-tuple-element.22) | data formatting | bytes 98304
  81.2 1.3 %copy.27 = f32[8,512]{1,0:T(8,128)} copy(f32[8,512]{1,0:T(8,128)} %get-tuple-element.23) | data formatting | bytes 32768

commit v2 on v1

v2 whole, which is shorter than its diff:
```python
import functools
import math

import jax
import jax.numpy as jnp
from jax import lax
from jax.experimental import pallas as pl
from jax.experimental.pallas import tpu as pltpu
from jax.sharding import PartitionSpec as P

MESH = pl.DeviceIdType.MESH
BF16 = jnp.bfloat16
F32 = jnp.float32

D = 512
HEADS = 16
PER_HEAD = D // HEADS
LV = 2
WLAT = 6
WLON = 12
CELLS = LV * WLAT * WLON
QUAD = CELLS // 4
SLAB = 48
EPS = 1e-05
SCALE = 1.0 / math.sqrt(PER_HEAD)
EXP2_SCALE = SCALE * math.log2(math.e)

NZ, NX, NYL = 8, 4, 2
PLANE = [(dx, dy) for dx in (2, 1, 3, 0) for dy in (2, 1, 3, 0) if (dx, dy) != (0, 0)]
COLUMN = [(dz, dh) for dz in (4, 3, 5, 2, 6, 1, 7, 0) for dh in (1, 0) if (dz, dh) != (0, 0)]


def mm(left, right):
    return lax.dot_general(left, right, (((1,), (0,)), ((), ())), preferred_element_type=F32)


def mm_nt(left, right):
    return lax.dot_general(left, right, (((1,), (1,)), ((), ())), preferred_element_type=F32)


def chunk_offset(row, side):
    quadrant = (0 if row >= 3 else 1) + (0 if side == 1 else 2)
    return quadrant * QUAD + row % 3 * 12


def field_to_cells(field_ref, cells_ref, change=lambda chunk, row, side: chunk):
    for row in range(WLAT):
        for side in range(2):
            off = chunk_offset(row, side)
            chunk = field_ref[row, side * 6 : side * 6 + 6, :, :].astype(F32)
            cells_ref[off : off + 12, :] = change(chunk, row, side).reshape(12, D)


def cells_to_field(cells_ref, field_ref):
    for row in range(WLAT):
        for side in range(2):
            off = chunk_offset(row, side)
            field_ref[row, side * 6 : side * 6 + 6, :, :] = cells_ref[off : off + 12, :].reshape(6, LV, D).astype(BF16)


def layer_norm(u):
    centre = jnp.mean(u, axis=-1, keepdims=True)
    centred = u - centre
    spread = lax.rsqrt(jnp.mean(centred * centred, axis=-1, keepdims=True) + EPS)
    return centred * spread, spread


def head_lanes(head):
    lane = lax.broadcasted_iota(jnp.int32, (CELLS, 256), 1)
    return (lane // PER_HEAD) == (head % 8)


def forward(blk, w_ref, wo_ref, mask_ref):
    u = blk.u[...]
    normed, spread = layer_norm(u)
    blk.normed[...] = normed
    blk.spread[...] = jnp.broadcast_to(spread, (CELLS, 128))
    hidden = normed.astype(BF16)
    blk.hid_t[...] = hidden.T
    for part in range(3):
        cols = slice(part * D, part * D + D)
        packed = mm(hidden, w_ref[:, cols]).astype(BF16)
        blk.pk[:, cols] = packed
        blk.pk_t[cols, :] = packed.T

    def one_head(head):
        group = head // 8
        q_g = blk.pk[:, group * 256 : group * 256 + 256]
        k_g = blk.pk[:, D + group * 256 : D + group * 256 + 256]
        k_h = jnp.where(head_lanes(head), k_g, jnp.zeros_like(k_g))
        weights = jnp.exp2(mm_nt(k_h, q_g) * EXP2_SCALE)
        if mask_ref is not None:
            weights = weights * mask_ref[...]
        attention = (weights * (1.0 / jnp.sum(weights, axis=0, keepdims=True))).astype(BF16)
        blk.att[head] = attention
        rows = slice(head * PER_HEAD, head * PER_HEAD + PER_HEAD)
        v_t = blk.pk_t[2 * D + head * PER_HEAD : 2 * D + head * PER_HEAD + PER_HEAD, :]
        blk.mix_t[rows, :] = mm(v_t, attention)

    for head in range(HEADS):
        one_head(head)
    mixed = blk.mix_t[...].astype(BF16).T
    return u + mm(mixed, wo_ref[...])


def head_rows(part, head):
    first = part * D + head * PER_HEAD
    return slice(first, first + PER_HEAD)


def backward_values(blk, wo_ref):
    dy_low = blk.dy[...].astype(BF16)
    blk.gm[...] = mm_nt(dy_low, wo_ref[...]).astype(BF16)
    blk.gm_t[...] = blk.gm[...].T
    for head in range(HEADS):
        g_t = blk.gm_t[head_rows(0, head), :]
        blk.dpk_t[head_rows(2, head), :] = mm_nt(g_t, blk.att[head]).astype(BF16)


def backward_scores(blk, heads):
    for head in heads:
        group = head // 8
        v_g = blk.pk[:, 2 * D + group * 256 : 2 * D + group * 256 + 256]
        g_g = blk.gm[:, group * 256 : group * 256 + 256]
        v_h = jnp.where(head_lanes(head), v_g, jnp.zeros_like(v_g))
        grad_attention = mm_nt(v_h, g_g)
        rows = head_rows(0, head)
        g_t = blk.gm_t[rows, :]
        inner = jnp.sum(blk.mix_t[rows, :] * g_t.astype(F32), axis=0, keepdims=True)
        grad_scores = (blk.att[head].astype(F32) * (grad_attention - inner)).astype(BF16)
        q_t = blk.pk_t[rows, :]
        k_t = blk.pk_t[head_rows(1, head), :]
        blk.dpk_t[rows, :] = (mm(k_t, grad_scores) * SCALE).astype(BF16)
        blk.dpk_t[head_rows(1, head), :] = (mm_nt(q_t, grad_scores) * SCALE).astype(BF16)


def backward_input(blk, w_ref):
    grad_hidden = mm(w_ref[...], blk.dpk_t[...]).T
    normed = blk.normed[...]
    spread = blk.spread[:, 0:1]
    return blk.dy[...] + spread * (
        grad_hidden
        - jnp.mean(grad_hidden, axis=-1, keepdims=True)
        - normed * jnp.mean(grad_hidden * normed, axis=-1, keepdims=True)
    )


def pack_unit(first, second):
    first = first.reshape(64, 8, D)
    second = second.reshape(64, 8, D)
    return jnp.concatenate([first, second], axis=1).astype(BF16).reshape(NZ, NX, NYL, 16, D)


def output_and_value_unit(blk):
    grad_output = mm(blk.mix_t[...].astype(BF16), blk.dy[...].astype(BF16))
    grad_value = mm_nt(blk.hid_t[...], blk.dpk_t[2 * D :, :])
    return pack_unit(grad_output, grad_value)


def query_and_key_unit(blk):
    hid_t = blk.hid_t[...]
    return pack_unit(mm_nt(hid_t, blk.dpk_t[0:D, :]), mm_nt(hid_t, blk.dpk_t[D : 2 * D, :]))


BLOCK_SCRATCH = (
    ("u", (CELLS, D), F32),
    ("normed", (CELLS, D), F32),
    ("spread", (CELLS, 128), F32),
    ("hid_t", (D, CELLS), BF16),
    ("pk", (CELLS, 3 * D), BF16),
    ("pk_t", (3 * D, CELLS), BF16),
    ("att", (HEADS, CELLS, CELLS), BF16),
    ("mix_t", (D, CELLS), F32),
    ("dy", (CELLS, D), F32),
    ("gm", (CELLS, D), BF16),
    ("gm_t", (D, CELLS), BF16),
    ("dpk_t", (3 * D, CELLS), BF16),
)


class Block:
    def __init__(self, refs):
        for (name, _, _), ref in zip(BLOCK_SCRATCH, refs):
            setattr(self, name, ref)


class Torus:
    def __init__(self):
        self.lat = lax.axis_index("lat")
        self.lon = lax.axis_index("lon")
        self.z = self.lat // 8
        self.x = (self.lat // 2) % 4
        self.y = (self.lon // 2) * 2 + self.lat % 2
        self.core = self.lon % 2

    def at(self, x=None, y=None, z=None, core=None):
        x = self.x if x is None else x
        y = self.y if y is None else y
        z = self.z if z is None else z
        core = self.core if core is None else core
        return (z * 8 + x * 2 + y % 2, (y // 2) * 2 + core)

    def shifted(self, dlat, dlon):
        return ((self.lat + dlat + 64) % 64, (self.lon + dlon + 4) % 4)

    def greeted(self):
        found = [self.shifted(*step) for step in ((1, 0), (-1, 0), (1, 1), (-1, -1), (0, 1), (0, -1))]
        found += [self.at(core=1 - self.core)]
        found += [self.in_plane(dx, dy) for dx, dy in PLANE]
        found += [self.in_column(dz, dh) for dz, dh in COLUMN]
        return found

    def in_plane(self, dx, dy):
        return self.at(x=(self.x + dx) % 4, y=(self.y + dy) % 4)

    def in_column(self, dz, dh):
        return self.at(z=(self.z + dz) % 8, y=(self.y + 2 * dh) % 4)


class Halo:
    STEPS = ((1, 0), (0, 1), (1, 1))

    def __init__(self, torus, index, sign, out_ref, in_ref, send_sem, recv_sem):
        self.out_ref = out_ref.at[index]
        self.in_ref = in_ref.at[index]
        self.copies = [
            pltpu.make_async_remote_copy(
                src_ref=out_ref.at[index, n],
                dst_ref=in_ref.at[index, n],
                send_sem=send_sem.at[index, n],
                recv_sem=recv_sem.at[index, n],
                device_id=torus.shifted(sign * step[0], sign * step[1]),
                device_id_type=MESH,
            )
            for n, step in enumerate(self.STEPS)
        ]

    def send(self, cells_ref):
        for n, copy in enumerate(self.copies):
            q = n + 1
            self.out_ref[n, 0:QUAD, :] = cells_ref[q * QUAD : q * QUAD + QUAD, :].astype(BF16)
            copy.start()

    def receive(self, cells_ref):
        for n, copy in enumerate(self.copies):
            q = n + 1
            copy.wait_recv()
            cells_ref[q * QUAD : q * QUAD + QUAD, :] = self.in_ref[n, 0:QUAD, :].astype(F32)

    def close(self):
        for copy in self.copies:
            copy.wait_send()


UNIT_SCRATCH = (
    ("whole", (NZ, NX, NYL, 16, D), BF16),
    ("core_in", (NZ, NX, NYL, 16, 256), BF16),
    ("half", (NZ, NX, NYL, 16, 256), BF16),
    ("last", (2, 2, 16, 128), F32),
)
PLANE_SCRATCH = UNIT_SCRATCH + (
    ("plane_in", (15, NZ, 16, 128), BF16),
    ("plane_sum", (NZ, 16, 128), BF16),
    ("column_in", (15, 16, 128), BF16),
)
Z_SCRATCH = UNIT_SCRATCH + (
    ("z_in", (7, NX, NYL, 16, 256), BF16),
    ("z_sum", (NX, NYL, 16, 256), BF16),
    ("plane_in", (15, 16, 256), BF16),
)
UNIT_SEMS = 32


class Unit:
    def __init__(self, torus, refs, send_sem, recv_sem):
        self.t = torus
        for (name, _, _), ref in zip(self.SCRATCH, refs):
            setattr(self, name, ref)
        self.send_sem, self.recv_sem = send_sem, recv_sem
        self.pending = []
        self.arriving = []

    def _copy(self, src, dst, sem, device):
        copy = pltpu.make_async_remote_copy(
            src_ref=src,
            dst_ref=dst,
            send_sem=self.send_sem.at[sem],
            recv_sem=self.recv_sem.at[sem],
            device_id=device,
            device_id_type=MESH,
        )
        copy.start()
        self.pending.append(copy)
        self.arriving.append(copy)

    def _arrived(self):
        for copy in self.arriving:
            copy.wait_recv()
        self.arriving = []

    def start(self):
        t = self.t
        cols = pl.ds(pl.multiple_of((1 - t.core) * 256, 256), 256)
        self._copy(self.whole.at[:, :, :, :, cols], self.core_in, 0, t.at(core=1 - t.core))

    def core_total(self):
        self._arrived()
        cols = pl.ds(pl.multiple_of(self.t.core * 256, 256), 256)
        self.half[...] = (self.whole[:, :, :, :, cols].astype(F32) + self.core_in[...].astype(F32)).astype(BF16)

    def send_last(self):
        t = self.t
        self._copy(self.last.at[t.core], self.last.at[t.core], 31, t.at(core=1 - t.core))

    def finish(self, first_ref, first_col, second_ref, second_col):
        self._arrived()
        for core in range(2):
            for high in range(2):
                off = core * 256 + high * 128
                first_ref[:, first_col + off : first_col + off + 128] = self.last[core, high, 0:8, :]
                second_ref[:, second_col + off : second_col + off + 128] = self.last[core, high, 8:16, :]

    def close(self):
        for copy in self.pending:
            copy.wait_send()


class PlaneUnit(Unit):
    SCRATCH = PLANE_SCRATCH

    def spread(self):
        t = self.t
        self.core_total()
        for dx, dy in PLANE:
            y = (t.y + dy) % 4
            cols = pl.ds(pl.multiple_of(y // 2 * 128, 128), 128)
            slot = (-dx) % 4 * 4 + (-dy) % 4 - 1
            self._copy(
                self.half.at[:, (t.x + dx) % 4, y % 2, :, cols], self.plane_in.at[slot], 1 + slot, t.in_plane(dx, dy)
            )

    def gather(self):
        t = self.t
        self._arrived()
        cols = pl.ds(pl.multiple_of(t.y // 2 * 128, 128), 128)
        total = self.half[:, t.x, t.y % 2, :, cols].astype(F32)
        for slot in range(15):
            total = total + self.plane_in[slot].astype(F32)
        self.plane_sum[...] = total.astype(BF16)
        for dz, dh in COLUMN:
            slot = (-dz) % 8 * 2 + dh - 1
            self._copy(self.plane_sum.at[(t.z + dz) % 8], self.column_in.at[slot], 16 + slot, t.in_column(dz, dh))

    def total(self):
        t = self.t
        self._arrived()
        mine = self.plane_sum[t.z].astype(F32)
        for dz in range(1, 8):
            mine = mine + self.column_in[dz * 2 - 1].astype(F32)
        other = self.column_in[0].astype(F32)
        for dz in range(1, 8):
            other = other + self.column_in[dz * 2].astype(F32)
        high = t.y // 2
        self.last[t.core, high] = mine
        self.last[t.core, 1 - high] = other
        self.send_last()


class ZUnit(Unit):
    SCRATCH = Z_SCRATCH

    def spread(self):
        t = self.t
        self.core_total()
        for dz in (4, 3, 5, 2, 6, 1, 7):
            self._copy(self.half.at[(t.z + dz) % 8], self.z_in.at[7 - dz], 8 - dz, t.in_column(dz, 0))

    def gather(self):
        t = self.t
        self._arrived()
        total = self.half[t.z].astype(F32)
        for slot in range(7):
            total = total + self.z_in[slot].astype(F32)
        self.z_sum[...] = total.astype(BF16)
        for dx, dy in PLANE:
            slot = (-dx) % 4 * 4 + (-dy) % 4 - 1
            self._copy(
                self.z_sum.at[(t.x + dx) % 4, (t.y + dy) % 2], self.plane_in.at[slot], 8 + slot, t.in_plane(dx, dy)
            )

    def total(self):
        t = self.t
        self._arrived()
        total = self.z_sum[t.x, t.y % 2].astype(F32)
        for slot in range(15):
            total = total + self.plane_in[slot].astype(F32)
        self.last[t.core, 0] = total[:, 0:128]
        self.last[t.core, 1] = total[:, 128:256]
        self.send_last()


UNIT_KINDS = (ZUnit, PlaneUnit, PlaneUnit, PlaneUnit)


def kernel(
    tokens_ref,
    land_ref,
    pole_ref,
    land_vec_ref,
    pole_vec_ref,
    w1_hbm,
    o1_hbm,
    w2_hbm,
    o2_hbm,
    cot_ref,
    layer_ref,
    tokens_grad_ref,
    ga1_ref,
    go1_ref,
    ga2_ref,
    go2_ref,
    *scratch,
):
    n = len(BLOCK_SCRATCH)
    one, two = Block(scratch[:n]), Block(scratch[n : 2 * n])
    rest = list(scratch[2 * n :])
    unit_refs = [[rest.pop(0) for _ in kind.SCRATCH] for kind in UNIT_KINDS]
    (w1_ref, o1_ref, w2_ref, o2_ref, cells_ref, mask_ref, halo_out, halo_in, load_sem, halo_send, halo_recv,
     red_send, red_recv) = rest

    torus = Torus()
    loads = [
        pltpu.make_async_copy(src, dst, load_sem.at[i])
        for i, (src, dst) in enumerate(((w1_hbm, w1_ref), (o1_hbm, o1_ref), (w2_hbm, w2_ref), (o2_hbm, o2_ref)))
    ]
    for load in loads:
        load.start()

    barrier = pltpu.get_barrier_semaphore()
    greeted = torus.greeted()
    for device in greeted:
        pl.semaphore_signal(barrier, inc=1, device_id=device, device_id_type=MESH)

    land = land_ref[...].astype(F32)
    at_cell = lax.broadcasted_iota(jnp.int32, (WLON, 1, WLON), 0)
    eye = at_cell == lax.broadcasted_iota(jnp.int32, (WLON, 1, WLON), 2)
    land_vec = land_vec_ref[...].astype(F32).reshape(1, 1, D)
    pole_vec = pole_vec_ref[...].astype(F32).reshape(1, 1, D)

    def mark(chunk, row, side):
        row_marks = jnp.broadcast_to(land[row : row + 1, :].reshape(1, 1, WLON), (WLON, 1, WLON))
        column = jnp.sum(jnp.where(eye, row_marks, 0.0), axis=2, keepdims=True)[side * 6 : side * 6 + 6]
        marked = chunk + column * land_vec + pole_ref[row].astype(F32) * pole_vec
        return marked.astype(BF16).astype(F32)

    field_to_cells(tokens_ref, one.u, mark)
    halos = [
        Halo(torus, i, sign, halo_out, halo_in, halo_send, halo_recv) for i, sign in enumerate((-1, -1, 1, 1))
    ]
    out2, query2, out1, query1 = (
        kind(torus, refs, red_send.at[i], red_recv.at[i]) for i, (kind, refs) in enumerate(zip(UNIT_KINDS, unit_refs))
    )

    loads[0].wait()
    loads[1].wait()
    first = forward(one, w1_ref, o1_ref, None)
    two.u[...] = first.astype(BF16).astype(F32)

    pl.semaphore_wait(barrier, len(greeted))
    halos[0].send(two.u)
    field_to_cells(cot_ref, two.dy)
    halos[1].send(two.dy)

    last = jnp.where(torus.lat == 63, 1.0, 0.0).astype(F32)
    far_k = (lax.broadcasted_iota(jnp.int32, (CELLS, CELLS), 0) // QUAD) % 2
    far_q = (lax.broadcasted_iota(jnp.int32, (CELLS, CELLS), 1) // QUAD) % 2
    mask_ref[...] = 1.0 - last * jnp.where(far_k == far_q, 0.0, 1.0)

    loads[2].wait()
    loads[3].wait()
    halos[0].receive(two.u)
    cells_ref[...] = forward(two, w2_ref, o2_ref, mask_ref)
    halos[2].send(cells_ref)
    halos[1].receive(two.dy)

    backward_values(two, o2_ref)
    backward_scores(two, range(HEADS))
    one.dy[...] = backward_input(two, w2_ref)
    halos[3].send(one.dy)
    out2.whole[...] = output_and_value_unit(two)
    out2.start()
    query2.whole[...] = query_and_key_unit(two)
    query2.start()
    out2.spread()
    query2.spread()

    halos[3].receive(one.dy)
    backward_values(one, o1_ref)
    out1.whole[...] = output_and_value_unit(one)
    out1.start()
    backward_scores(one, range(HEADS // 2))
    out1.spread()
    backward_scores(one, range(HEADS // 2, HEADS))
    query1.whole[...] = query_and_key_unit(one)
    query1.start()
    query1.spread()

    halos[2].receive(cells_ref)
    cells_to_field(cells_ref, layer_ref)
    cells_ref[...] = backward_input(one, w1_ref)
    cells_to_field(cells_ref, tokens_grad_ref)

    query2.gather()
    out1.gather()
    out2.gather()
    query1.gather()
    query2.total()
    out1.total()
    out2.total()
    query2.finish(ga2_ref, 0, ga2_ref, D)
    out2.finish(go2_ref, 0, ga2_ref, 2 * D)
    out1.finish(go1_ref, 0, ga1_ref, 2 * D)
    query1.total()
    query1.finish(ga1_ref, 0, ga1_ref, D)
    for each in halos + [out2, query2, out1, query1]:
        each.close()


def hand_over(*refs):
    for i in range(6):
        refs[6 + i][...] = refs[i][...]


def local(
    tokens,
    land_sea,
    pole_band,
    land_embedding,
    pole_embedding,
    attend_first,
    output_first,
    attend_second,
    output_second,
    cotangent,
):
    vmem = pl.BlockSpec(memory_space=pltpu.VMEM)
    smem = pl.BlockSpec(memory_space=pltpu.SMEM)
    hbm = pl.BlockSpec(memory_space=pl.ANY)
    field = jax.ShapeDtypeStruct((WLAT, WLON, LV, D), BF16)
    shapes = (
        field,
        field,
        jax.ShapeDtypeStruct((8, 3 * D), F32),
        jax.ShapeDtypeStruct((8, D), F32),
        jax.ShapeDtypeStruct((8, 3 * D), F32),
        jax.ShapeDtypeStruct((8, D), F32),
    )
    results = pl.pallas_call(
        kernel,
        out_shape=shapes,
        in_specs=[vmem, vmem, smem, vmem, vmem, hbm, hbm, hbm, hbm, vmem],
        out_specs=[vmem] * 6,
        scratch_shapes=[pltpu.VMEM(shape, dtype) for _, shape, dtype in BLOCK_SCRATCH * 2 + sum((k.SCRATCH for k in UNIT_KINDS), ())]
        + [
            pltpu.VMEM((D, 3 * D), BF16),
            pltpu.VMEM((D, D), BF16),
            pltpu.VMEM((D, 3 * D), BF16),
            pltpu.VMEM((D, D), BF16),
            pltpu.VMEM((CELLS, D), F32),
            pltpu.VMEM((CELLS, CELLS), F32),
            pltpu.VMEM((4, 3, SLAB, D), BF16),
            pltpu.VMEM((4, 3, SLAB, D), BF16),
            pltpu.SemaphoreType.DMA((4,)),
            pltpu.SemaphoreType.DMA((4, 3)),
            pltpu.SemaphoreType.DMA((4, 3)),
            pltpu.SemaphoreType.DMA((4, UNIT_SEMS)),
            pltpu.SemaphoreType.DMA((4, UNIT_SEMS)),
        ],
        compiler_params=pltpu.CompilerParams(
            collective_id=0, has_side_effects=True, vmem_limit_bytes=56 * 1024 * 1024
        ),
    )(
        tokens.transpose(1, 2, 0, 3),
        land_sea,
        pole_band,
        land_embedding,
        pole_embedding,
        attend_first,
        output_first,
        attend_second,
        output_second,
        cotangent.transpose(1, 2, 0, 3),
    )
    results = pl.pallas_call(
        hand_over,
        out_shape=shapes,
        in_specs=[vmem] * 6,
        out_specs=[vmem] * 6,
    )(*results)
    return tuple(r.transpose(2, 0, 1, 3) for r in results[:2]) + tuple(results[2:])


def solution(mesh):
    placed = (
        P(None, "lat", "lon", None),
        P("lat", "lon"),
        P("lat"),
        P(),
        P(),
        P(),
        P(),
        P(),
        P(),
        P(None, "lat", "lon", None),
    )
    return jax.shard_map(
        local,
        mesh=mesh,
        in_specs=placed,
        out_specs=(
            P(None, "lat", "lon", None),
            P(None, "lat", "lon", None),
            P("lat", None),
            P("lat", None),
            P("lat", None),
            P("lat", None),
        ),
        check_vma=False,
    )
```

time: 83.1 us -> 64.2 us (0.77)
  local copies, waits for them, and re-layouts: 14.7 us -> 0 us
  Pallas kernels: 67.2 us -> 63.2 us
    unnamed x6 -> x0, local copies, waits for them, and re-layouts: 8.71 us -> none
    pallas_call x1 -> x2, Pallas kernels: 67.2 us -> 63.2 us  [the longest x1 61.4 us: local(): pl.pallas_call(kernel, out_shape=shapes, in_specs=[vmem, vmem, smem, vmem...]
    pallas_call x2 -> x0, local copies, waits for them, and re-layouts: 3.48 us -> none  [local(): pl.pallas_call(kernel, out_shape=(field, field, jax.ShapeDtypeStruct((8,...]
    reshape x2 -> x0, local copies, waits for them, and re-layouts: 2.52 us -> none  [the longest x1 1.26 us: local(): land_embedding.reshape(1, D)]
where the time goes in v2:
time: 64.2 us; the launch traced here: 63.9 us
  Pallas kernels  63.2 us (98%)
    pallas_call x1, Pallas kernels, local(): pl.pallas_call(kernel, out_shape=shapes, in_specs=[vmem, vmem, smem, vmem...  61.4 us
    pallas_call x1, Pallas kernels, local(): pl.pallas_call(hand_over, out_shape=shapes, in_specs=[vmem] * 6, out_spec...  1.76 us

profile of v2, /device:TPU:1, one launch (start us, length us, event | category | flops | bytes accessed | tf_op | source)
XLA Modules:
  0.0 63.9 jit_solution(9101517401240548988)
XLA Ops:
  0.6 61.4 %shard_map.145 = (bf16[6,12,2,512]{3,2,1,0:T(2,128)(2,1)}, bf16[6,12,2,512]{3,2,1,0:T(2,128)(2,1)}, f32[8,1536]{1,0:T(8,128)}, f32[8,512]{1,0:T(8,128)}, f32[8,1536]{1,0:T(8,128)}, /*index=5*/f32[8,512]{1,0:T(8,128)}) custom-call(bf16[6,12,2,512]{3,2,1,0:T(2,128)(2,1)} %bitcast.4, s32[6,12]{1,0:T(8,128)} %land_ref.1, s32[6]{0:T(128)} %pole_ref.1, ...), custom_call_target="tpu_custom_call" | custom-call | tf_op jit(solution)/shard_map/pallas_call | solution.py:558
  62.1 1.8 %shard_map.146 = (bf16[6,12,2,512]{3,2,1,0:T(2,128)(2,1)}, bf16[6,12,2,512]{3,2,1,0:T(2,128)(2,1)}, f32[8,1536]{1,0:T(8,128)}, f32[8,512]{1,0:T(8,128)}, f32[8,1536]{1,0:T(8,128)}, /*index=5*/f32[8,512]{1,0:T(8,128)}) custom-call(bf16[6,12,2,512]{3,2,1,0:T(2,128)(2,1)} %get-tuple-element.18.refs_0_, bf16[6,12,2,512]{3,2,1,0:T(2,128)(2,1)} %get-tuple-element.19.refs_1_, ...), custom_call_target="tpu_custom_call" | custom-call | tf_op jit(solution)/shard_map/pallas_call | solution.py:594

commit v3 on v2

--- a/solution.py
+++ b/solution.py
@@ -70,6 +70,11 @@
     return (lane // PER_HEAD) == (head % 8)
 
 
+def head_rows(part, head):
+    first = part * D + head * PER_HEAD
+    return slice(first, first + PER_HEAD)
+
+
 def forward(blk, w_ref, wo_ref, mask_ref):
     u = blk.u[...]
     normed, spread = layer_norm(u)
@@ -93,25 +98,22 @@
             weights = weights * mask_ref[...]
         attention = (weights * (1.0 / jnp.sum(weights, axis=0, keepdims=True))).astype(BF16)
         blk.att[head] = attention
-        rows = slice(head * PER_HEAD, head * PER_HEAD + PER_HEAD)
-        v_t = blk.pk_t[2 * D + head * PER_HEAD : 2 * D + head * PER_HEAD + PER_HEAD, :]
-        blk.mix_t[rows, :] = mm(v_t, attention)
 
     for head in range(HEADS):
         one_head(head)
+    for head in range(HEADS):
+        blk.mix_t[head_rows(0, head), :] = mm(blk.pk_t[head_rows(2, head), :], blk.att[head])
     mixed = blk.mix_t[...].astype(BF16).T
     return u + mm(mixed, wo_ref[...])
 
 
-def head_rows(part, head):
-    first = part * D + head * PER_HEAD
-    return slice(first, first + PER_HEAD)
-
-
-def backward_values(blk, wo_ref):
+def backward_mixed(blk, wo_ref):
     dy_low = blk.dy[...].astype(BF16)
     blk.gm[...] = mm_nt(dy_low, wo_ref[...]).astype(BF16)
     blk.gm_t[...] = blk.gm[...].T
+
+
+def backward_values(blk):
     for head in range(HEADS):
         g_t = blk.gm_t[head_rows(0, head), :]
         blk.dpk_t[head_rows(2, head), :] = mm_nt(g_t, blk.att[head]).astype(BF16)
@@ -125,13 +127,13 @@
         v_h = jnp.where(head_lanes(head), v_g, jnp.zeros_like(v_g))
         grad_attention = mm_nt(v_h, g_g)
         rows = head_rows(0, head)
-        g_t = blk.gm_t[rows, :]
-        inner = jnp.sum(blk.mix_t[rows, :] * g_t.astype(F32), axis=0, keepdims=True)
-        grad_scores = (blk.att[head].astype(F32) * (grad_attention - inner)).astype(BF16)
-        q_t = blk.pk_t[rows, :]
-        k_t = blk.pk_t[head_rows(1, head), :]
-        blk.dpk_t[rows, :] = (mm(k_t, grad_scores) * SCALE).astype(BF16)
-        blk.dpk_t[head_rows(1, head), :] = (mm_nt(q_t, grad_scores) * SCALE).astype(BF16)
+        inner = jnp.sum(blk.mix_t[rows, :] * blk.gm_t[rows, :].astype(F32), axis=0, keepdims=True)
+        blk.dsc[head] = (blk.att[head].astype(F32) * (grad_attention - inner)).astype(BF16)
+    for head in heads:
+        rows, key_rows = head_rows(0, head), head_rows(1, head)
+        grad_scores = blk.dsc[head]
+        blk.dpk_t[rows, :] = (mm(blk.pk_t[key_rows, :], grad_scores) * SCALE).astype(BF16)
+        blk.dpk_t[key_rows, :] = (mm_nt(blk.pk_t[rows, :], grad_scores) * SCALE).astype(BF16)
 
 
 def backward_input(blk, w_ref):
@@ -170,6 +172,7 @@
     ("pk", (CELLS, 3 * D), BF16),
     ("pk_t", (3 * D, CELLS), BF16),
     ("att", (HEADS, CELLS, CELLS), BF16),
+    ("dsc", (HEADS, CELLS, CELLS), BF16),
     ("mix_t", (D, CELLS), F32),
     ("dy", (CELLS, D), F32),
     ("gm", (CELLS, D), BF16),
@@ -217,39 +220,39 @@
         return self.at(z=(self.z + dz) % 8, y=(self.y + 2 * dh) % 4)
 
 
+def wait_all(ref, sem):
+    pltpu.make_async_copy(ref, ref, sem).wait()
+
+
 class Halo:
     STEPS = ((1, 0), (0, 1), (1, 1))
 
     def __init__(self, torus, index, sign, out_ref, in_ref, send_sem, recv_sem):
-        self.out_ref = out_ref.at[index]
-        self.in_ref = in_ref.at[index]
-        self.copies = [
-            pltpu.make_async_remote_copy(
-                src_ref=out_ref.at[index, n],
-                dst_ref=in_ref.at[index, n],
-                send_sem=send_sem.at[index, n],
-                recv_sem=recv_sem.at[index, n],
-                device_id=torus.shifted(sign * step[0], sign * step[1]),
-                device_id_type=MESH,
-            )
-            for n, step in enumerate(self.STEPS)
-        ]
+        self.torus, self.sign = torus, sign
+        self.out_ref, self.in_ref = out_ref.at[index], in_ref.at[index]
+        self.send_sem, self.recv_sem = send_sem.at[index], recv_sem.at[index]
 
     def send(self, cells_ref):
-        for n, copy in enumerate(self.copies):
+        for n, (dlat, dlon) in enumerate(self.STEPS):
             q = n + 1
             self.out_ref[n, 0:QUAD, :] = cells_ref[q * QUAD : q * QUAD + QUAD, :].astype(BF16)
-            copy.start()
+            pltpu.make_async_remote_copy(
+                src_ref=self.out_ref.at[n],
+                dst_ref=self.in_ref.at[n],
+                send_sem=self.send_sem,
+                recv_sem=self.recv_sem,
+                device_id=self.torus.shifted(self.sign * dlat, self.sign * dlon),
+                device_id_type=MESH,
+            ).start()
 
     def receive(self, cells_ref):
-        for n, copy in enumerate(self.copies):
+        wait_all(self.in_ref, self.recv_sem)
+        for n in range(3):
             q = n + 1
-            copy.wait_recv()
             cells_ref[q * QUAD : q * QUAD + QUAD, :] = self.in_ref[n, 0:QUAD, :].astype(F32)
 
     def close(self):
-        for copy in self.copies:
-            copy.wait_send()
+        wait_all(self.out_ref, self.send_sem)
 
 
 UNIT_SCRATCH = (
@@ -260,15 +263,14 @@
 )
 PLANE_SCRATCH = UNIT_SCRATCH + (
     ("plane_in", (15, NZ, 16, 128), BF16),
-    ("plane_sum", (NZ, 16, 128), BF16),
-    ("column_in", (15, 16, 128), BF16),
 )
 Z_SCRATCH = UNIT_SCRATCH + (
     ("z_in", (7, NX, NYL, 16, 256), BF16),
     ("z_sum", (NX, NYL, 16, 256), BF16),
     ("plane_in", (15, 16, 256), BF16),
 )
-UNIT_SEMS = 32
+UNIT_SEMS = 4
+CORE, MIDDLE, PLANE_LATE, LAST = range(UNIT_SEMS)
 
 
 class Unit:
@@ -277,43 +279,38 @@
         for (name, _, _), ref in zip(self.SCRATCH, refs):
             setattr(self, name, ref)
         self.send_sem, self.recv_sem = send_sem, recv_sem
-        self.pending = []
-        self.arriving = []
-
-    def _copy(self, src, dst, sem, device):
-        copy = pltpu.make_async_remote_copy(
+        self.sent = []
+
+    def _copy(self, src, dst, stage, device):
+        pltpu.make_async_remote_copy(
             src_ref=src,
             dst_ref=dst,
-            send_sem=self.send_sem.at[sem],
-            recv_sem=self.recv_sem.at[sem],
+            send_sem=self.send_sem.at[stage],
+            recv_sem=self.recv_sem.at[stage],
             device_id=device,
             device_id_type=MESH,
-        )
-        copy.start()
-        self.pending.append(copy)
-        self.arriving.append(copy)
-
-    def _arrived(self):
-        for copy in self.arriving:
-            copy.wait_recv()
-        self.arriving = []
+        ).start()
+
+    def _arrived(self, stage, ref):
+        wait_all(ref, self.recv_sem.at[stage])
+        self.sent.append((stage, ref))
 
     def start(self):
         t = self.t
         cols = pl.ds(pl.multiple_of((1 - t.core) * 256, 256), 256)
-        self._copy(self.whole.at[:, :, :, :, cols], self.core_in, 0, t.at(core=1 - t.core))
+        self._copy(self.whole.at[:, :, :, :, cols], self.core_in, CORE, t.at(core=1 - t.core))
 
     def core_total(self):
-        self._arrived()
+        self._arrived(CORE, self.core_in)
         cols = pl.ds(pl.multiple_of(self.t.core * 256, 256), 256)
         self.half[...] = (self.whole[:, :, :, :, cols].astype(F32) + self.core_in[...].astype(F32)).astype(BF16)
 
     def send_last(self):
         t = self.t
-        self._copy(self.last.at[t.core], self.last.at[t.core], 31, t.at(core=1 - t.core))
+        self._copy(self.last.at[t.core], self.last.at[t.core], LAST, t.at(core=1 - t.core))
 
     def finish(self, first_ref, first_col, second_ref, second_col):
-        self._arrived()
+        self._arrived(LAST, self.last.at[1 - self.t.core])
         for core in range(2):
             for high in range(2):
                 off = core * 256 + high * 128
@@ -321,8 +318,8 @@
                 second_ref[:, second_col + off : second_col + off + 128] = self.last[core, high, 8:16, :]
 
     def close(self):
-        for copy in self.pending:
-            copy.wait_send()
+        for stage, ref in self.sent:
+            wait_all(ref, self.send_sem.at[stage])
 
 
 class PlaneUnit(Unit):
@@ -336,34 +333,54 @@
             cols = pl.ds(pl.multiple_of(y // 2 * 128, 128), 128)
             slot = (-dx) % 4 * 4 + (-dy) % 4 - 1
             self._copy(
-                self.half.at[:, (t.x + dx) % 4, y % 2, :, cols], self.plane_in.at[slot], 1 + slot, t.in_plane(dx, dy)
+                self.half.at[:, (t.x + dx) % 4, y % 2, :, cols], self.plane_in.at[slot], MIDDLE, t.in_plane(dx, dy)
             )
 
-    def gather(self):
-        t = self.t
-        self._arrived()
+    def plane_total(self, sum_ref, place):
+        t = self.t
+        self._arrived(MIDDLE, self.plane_in)
         cols = pl.ds(pl.multiple_of(t.y // 2 * 128, 128), 128)
         total = self.half[:, t.x, t.y % 2, :, cols].astype(F32)
         for slot in range(15):
             total = total + self.plane_in[slot].astype(F32)
-        self.plane_sum[...] = total.astype(BF16)
+        sum_ref[:, place] = total.astype(BF16)
+
+
+class Column:
+    def __init__(self, torus, units, sum_ref, in_ref, send_sem, recv_sem):
+        self.t, self.units, self.sum, self.came = torus, units, sum_ref, in_ref
+        self.send_sem, self.recv_sem = send_sem, recv_sem
+
+    def send(self):
+        t = self.t
         for dz, dh in COLUMN:
             slot = (-dz) % 8 * 2 + dh - 1
-            self._copy(self.plane_sum.at[(t.z + dz) % 8], self.column_in.at[slot], 16 + slot, t.in_column(dz, dh))
+            pltpu.make_async_remote_copy(
+                src_ref=self.sum.at[(t.z + dz) % 8],
+                dst_ref=self.came.at[slot],
+                send_sem=self.send_sem,
+                recv_sem=self.recv_sem,
+                device_id=t.in_column(dz, dh),
+                device_id_type=MESH,
+            ).start()
 
     def total(self):
         t = self.t
-        self._arrived()
-        mine = self.plane_sum[t.z].astype(F32)
+        wait_all(self.came, self.recv_sem)
+        mine = self.sum[t.z].astype(F32)
         for dz in range(1, 8):
-            mine = mine + self.column_in[dz * 2 - 1].astype(F32)
-        other = self.column_in[0].astype(F32)
+            mine = mine + self.came[dz * 2 - 1].astype(F32)
+        other = self.came[0].astype(F32)
         for dz in range(1, 8):
-            other = other + self.column_in[dz * 2].astype(F32)
+            other = other + self.came[dz * 2].astype(F32)
         high = t.y // 2
-        self.last[t.core, high] = mine
-        self.last[t.core, 1 - high] = other
-        self.send_last()
+        for place, unit in enumerate(self.units):
+            unit.last[t.core, high] = mine[place]
+            unit.last[t.core, 1 - high] = other[place]
+            unit.send_last()
+
+    def close(self):
+        wait_all(self.came, self.send_sem)
 
 
 class ZUnit(Unit):
@@ -373,11 +390,11 @@
         t = self.t
         self.core_total()
         for dz in (4, 3, 5, 2, 6, 1, 7):
-            self._copy(self.half.at[(t.z + dz) % 8], self.z_in.at[7 - dz], 8 - dz, t.in_column(dz, 0))
+            self._copy(self.half.at[(t.z + dz) % 8], self.z_in.at[7 - dz], MIDDLE, t.in_column(dz, 0))
 
     def gather(self):
         t = self.t
-        self._arrived()
+        self._arrived(MIDDLE, self.z_in)
         total = self.half[t.z].astype(F32)
         for slot in range(7):
             total = total + self.z_in[slot].astype(F32)
@@ -385,12 +402,12 @@
         for dx, dy in PLANE:
             slot = (-dx) % 4 * 4 + (-dy) % 4 - 1
             self._copy(
-                self.z_sum.at[(t.x + dx) % 4, (t.y + dy) % 2], self.plane_in.at[slot], 8 + slot, t.in_plane(dx, dy)
+                self.z_sum.at[(t.x + dx) % 4, (t.y + dy) % 2], self.plane_in.at[slot], PLANE_LATE, t.in_plane(dx, dy)
             )
 
     def total(self):
         t = self.t
-        self._arrived()
+        self._arrived(PLANE_LATE, self.plane_in)
         total = self.z_sum[t.x, t.y % 2].astype(F32)
         for slot in range(15):
             total = total + self.plane_in[slot].astype(F32)
@@ -403,16 +420,16 @@
 
 
 def kernel(
-    tokens_ref,
-    land_ref,
+    tokens_hbm,
+    land_hbm,
     pole_ref,
-    land_vec_ref,
-    pole_vec_ref,
+    land_vec_hbm,
+    pole_vec_hbm,
     w1_hbm,
     o1_hbm,
     w2_hbm,
     o2_hbm,
-    cot_ref,
+    cot_hbm,
     layer_ref,
     tokens_grad_ref,
     ga1_ref,
@@ -425,13 +442,26 @@
     one, two = Block(scratch[:n]), Block(scratch[n : 2 * n])
     rest = list(scratch[2 * n :])
     unit_refs = [[rest.pop(0) for _ in kind.SCRATCH] for kind in UNIT_KINDS]
-    (w1_ref, o1_ref, w2_ref, o2_ref, cells_ref, mask_ref, halo_out, halo_in, load_sem, halo_send, halo_recv,
-     red_send, red_recv) = rest
+    (tokens_ref, cot_ref, land_ref, land_vec_ref, pole_vec_ref, w1_ref, o1_ref, w2_ref, o2_ref, cells_ref, mask_ref,
+     sum2, sum1, came2, came1, halo_out, halo_in, load_sem, halo_send, halo_recv, red_send, red_recv, col_send,
+     col_recv) = rest
 
     torus = Torus()
     loads = [
         pltpu.make_async_copy(src, dst, load_sem.at[i])
-        for i, (src, dst) in enumerate(((w1_hbm, w1_ref), (o1_hbm, o1_ref), (w2_hbm, w2_ref), (o2_hbm, o2_ref)))
+        for i, (src, dst) in enumerate(
+            (
+                (tokens_hbm, tokens_ref),
+                (land_hbm, land_ref),
+                (land_vec_hbm, land_vec_ref),
+                (pole_vec_hbm, pole_vec_ref),
+                (w1_hbm, w1_ref),
+                (o1_hbm, o1_ref),
+                (cot_hbm, cot_ref),
+                (w2_hbm, w2_ref),
+                (o2_hbm, o2_ref),
+            )
+        )
     ]
     for load in loads:
         load.start()
@@ -441,6 +471,8 @@
     for device in greeted:
         pl.semaphore_signal(barrier, inc=1, device_id=device, device_id_type=MESH)
 
+    for load in loads[:4]:
+        load.wait()
     land = land_ref[...].astype(F32)
     at_cell = lax.broadcasted_iota(jnp.int32, (WLON, 1, WLON), 0)
     eye = at_cell == lax.broadcasted_iota(jnp.int32, (WLON, 1, WLON), 2)
@@ -460,14 +492,17 @@
     out2, query2, out1, query1 = (
         kind(torus, refs, red_send.at[i], red_recv.at[i]) for i, (kind, refs) in enumerate(zip(UNIT_KINDS, unit_refs))
     )
-
-    loads[0].wait()
-    loads[1].wait()
+    column2 = Column(torus, [query2], sum2, came2, col_send.at[0], col_recv.at[0])
+    column1 = Column(torus, [query1, out1], sum1, came1, col_send.at[1], col_recv.at[1])
+
+    loads[4].wait()
+    loads[5].wait()
     first = forward(one, w1_ref, o1_ref, None)
     two.u[...] = first.astype(BF16).astype(F32)
 
     pl.semaphore_wait(barrier, len(greeted))
     halos[0].send(two.u)
+    loads[6].wait()
     field_to_cells(cot_ref, two.dy)
     halos[1].send(two.dy)
 
@@ -476,14 +511,15 @@
     far_q = (lax.broadcasted_iota(jnp.int32, (CELLS, CELLS), 1) // QUAD) % 2
     mask_ref[...] = 1.0 - last * jnp.where(far_k == far_q, 0.0, 1.0)
 
-    loads[2].wait()
-    loads[3].wait()
+    loads[7].wait()
+    loads[8].wait()
     halos[0].receive(two.u)
     cells_ref[...] = forward(two, w2_ref, o2_ref, mask_ref)
     halos[2].send(cells_ref)
     halos[1].receive(two.dy)
 
-    backward_values(two, o2_ref)
+    backward_mixed(two, o2_ref)
+    backward_values(two)
     backward_scores(two, range(HEADS))
     one.dy[...] = backward_input(two, w2_ref)
     halos[3].send(one.dy)
@@ -495,14 +531,14 @@
     query2.spread()
 
     halos[3].receive(one.dy)
-    backward_values(one, o1_ref)
+    backward_mixed(one, o1_ref)
+    backward_values(one)
     out1.whole[...] = output_and_value_unit(one)
     out1.start()
-    backward_scores(one, range(HEADS // 2))
-    out1.spread()
-    backward_scores(one, range(HEADS // 2, HEADS))
+    backward_scores(one, range(HEADS))
     query1.whole[...] = query_and_key_unit(one)
     query1.start()
+    out1.spread()
     query1.spread()
 
     halos[2].receive(cells_ref)
@@ -510,19 +546,20 @@
     cells_ref[...] = backward_input(one, w1_ref)
     cells_to_field(cells_ref, tokens_grad_ref)
 
-    query2.gather()
-    out1.gather()
+    query2.plane_total(sum2, 0)
+    column2.send()
     out2.gather()
-    query1.gather()
-    query2.total()
-    out1.total()
+    out1.plane_total(sum1, 1)
+    query1.plane_total(sum1, 0)
+    column1.send()
+    column2.total()
     out2.total()
     query2.finish(ga2_ref, 0, ga2_ref, D)
     out2.finish(go2_ref, 0, ga2_ref, 2 * D)
+    column1.total()
+    query1.finish(ga1_ref, 0, ga1_ref, D)
     out1.finish(go1_ref, 0, ga1_ref, 2 * D)
-    query1.total()
-    query1.finish(ga1_ref, 0, ga1_ref, D)
-    for each in halos + [out2, query2, out1, query1]:
+    for each in halos + [out2, query2, out1, query1, column2, column1]:
         each.close()
 
 
@@ -558,23 +595,34 @@
     results = pl.pallas_call(
         kernel,
         out_shape=shapes,
-        in_specs=[vmem, vmem, smem, vmem, vmem, hbm, hbm, hbm, hbm, vmem],
+        in_specs=[hbm, hbm, smem, hbm, hbm, hbm, hbm, hbm, hbm, hbm],
         out_specs=[vmem] * 6,
         scratch_shapes=[pltpu.VMEM(shape, dtype) for _, shape, dtype in BLOCK_SCRATCH * 2 + sum((k.SCRATCH for k in UNIT_KINDS), ())]
         + [
+            pltpu.VMEM((WLAT, WLON, LV, D), BF16),
+            pltpu.VMEM((WLAT, WLON, LV, D), BF16),
+            pltpu.VMEM((WLAT, WLON), jnp.int32),
+            pltpu.VMEM((D,), BF16),
+            pltpu.VMEM((D,), BF16),
             pltpu.VMEM((D, 3 * D), BF16),
             pltpu.VMEM((D, D), BF16),
             pltpu.VMEM((D, 3 * D), BF16),
             pltpu.VMEM((D, D), BF16),
             pltpu.VMEM((CELLS, D), F32),
             pltpu.VMEM((CELLS, CELLS), F32),
+            pltpu.VMEM((NZ, 1, 16, 128), BF16),
+            pltpu.VMEM((NZ, 2, 16, 128), BF16),
+            pltpu.VMEM((15, 1, 16, 128), BF16),
+            pltpu.VMEM((15, 2, 16, 128), BF16),
             pltpu.VMEM((4, 3, SLAB, D), BF16),
             pltpu.VMEM((4, 3, SLAB, D), BF16),
+            pltpu.SemaphoreType.DMA((9,)),
             pltpu.SemaphoreType.DMA((4,)),
-            pltpu.SemaphoreType.DMA((4, 3)),
-            pltpu.SemaphoreType.DMA((4, 3)),
+            pltpu.SemaphoreType.DMA((4,)),
             pltpu.SemaphoreType.DMA((4, UNIT_SEMS)),
             pltpu.SemaphoreType.DMA((4, UNIT_SEMS)),
+            pltpu.SemaphoreType.DMA((2,)),
+            pltpu.SemaphoreType.DMA((2,)),
         ],
         compiler_params=pltpu.CompilerParams(
             collective_id=0, has_side_effects=True, vmem_limit_bytes=56 * 1024 * 1024

time: 64.2 us -> 57 us (0.89)
  Pallas kernels: 63.2 us -> 55.8 us
    pallas_call x1, Pallas kernels: 61.4 us -> 54.1 us  [local(): pl.pallas_call(kernel, out_shape=shapes, in_specs=[hbm, hbm, smem, hbm, h...]
where the time goes in v3:
time: 57 us; the launch traced here: 56.5 us
  Pallas kernels  55.8 us (98%)
  between operations  0.64 us (1%)
    pallas_call x1, Pallas kernels, local(): pl.pallas_call(kernel, out_shape=shapes, in_specs=[hbm, hbm, smem, hbm, h...  54.1 us
    pallas_call x1, Pallas kernels, local(): pl.pallas_call(hand_over, out_shape=shapes, in_specs=[vmem] * 6, out_spec...  1.76 us

profile of v3, /device:TPU:1, one launch (start us, length us, event | category | flops | bytes accessed | tf_op | source)
XLA Modules:
  0.0 56.5 jit_solution(16408560569516215828)
XLA Ops:
  0.6 54.1 %shard_map.145 = (bf16[6,12,2,512]{3,2,1,0:T(2,128)(2,1)}, bf16[6,12,2,512]{3,2,1,0:T(2,128)(2,1)}, f32[8,1536]{1,0:T(8,128)}, f32[8,512]{1,0:T(8,128)}, f32[8,1536]{1,0:T(8,128)}, /*index=5*/f32[8,512]{1,0:T(8,128)}) custom-call(bf16[6,12,2,512]{3,2,1,0:T(2,128)(2,1)} %bitcast.4, s32[6,12]{1,0:T(8,128)} %land_hbm.1, s32[6]{0:T(128)} %pole_ref.1, ...), custom_call_target="tpu_custom_call" | custom-call | tf_op jit(solution)/shard_map/pallas_call | solution.py:595
  54.7 1.8 %shard_map.146 = (bf16[6,12,2,512]{3,2,1,0:T(2,128)(2,1)}, bf16[6,12,2,512]{3,2,1,0:T(2,128)(2,1)}, f32[8,1536]{1,0:T(8,128)}, f32[8,512]{1,0:T(8,128)}, f32[8,1536]{1,0:T(8,128)}, /*index=5*/f32[8,512]{1,0:T(8,128)}) custom-call(bf16[6,12,2,512]{3,2,1,0:T(2,128)(2,1)} %get-tuple-element.18.refs_0_, bf16[6,12,2,512]{3,2,1,0:T(2,128)(2,1)} %get-tuple-element.19.refs_1_, ...), custom_call_target="tpu_custom_call" | custom-call | tf_op jit(solution)/shard_map/pallas_call | solution.py:642

commit v4 on v3

--- a/solution.py
+++ b/solution.py
@@ -26,7 +26,6 @@
 EXP2_SCALE = SCALE * math.log2(math.e)
 
 NZ, NX, NYL = 8, 4, 2
-PLANE = [(dx, dy) for dx in (2, 1, 3, 0) for dy in (2, 1, 3, 0) if (dx, dy) != (0, 0)]
 COLUMN = [(dz, dh) for dz in (4, 3, 5, 2, 6, 1, 7, 0) for dh in (1, 0) if (dz, dh) != (0, 0)]
 
 
@@ -209,7 +208,7 @@
     def greeted(self):
         found = [self.shifted(*step) for step in ((1, 0), (-1, 0), (1, 1), (-1, -1), (0, 1), (0, -1))]
         found += [self.at(core=1 - self.core)]
-        found += [self.in_plane(dx, dy) for dx, dy in PLANE]
+        found += [self.in_plane(*step) for step in ((2, 0), (0, 2), (1, 0), (3, 0), (0, 1), (0, 3))]
         found += [self.in_column(dz, dh) for dz, dh in COLUMN]
         return found
 
@@ -261,22 +260,22 @@
     ("half", (NZ, NX, NYL, 16, 256), BF16),
     ("last", (2, 2, 16, 128), F32),
 )
-PLANE_SCRATCH = UNIT_SCRATCH + (
-    ("plane_in", (15, NZ, 16, 128), BF16),
+STEP_SCRATCH = UNIT_SCRATCH + (
+    ("x_in", (3, 4, NYL, 16, 256), BF16),
+    ("x_sum", (4, NYL, 16, 256), BF16),
+    ("y_in", (3, 4, NX, 16, 128), BF16),
+    ("y_sum", (4, NX, 16, 128), BF16),
+    ("xy_in", (3, 4, 16, 128), BF16),
+    ("yx_in", (3, 4, 16, 128), BF16),
 )
-Z_SCRATCH = UNIT_SCRATCH + (
-    ("z_in", (7, NX, NYL, 16, 256), BF16),
-    ("z_sum", (NX, NYL, 16, 256), BF16),
-    ("plane_in", (15, 16, 256), BF16),
-)
-UNIT_SEMS = 4
-CORE, MIDDLE, PLANE_LATE, LAST = range(UNIT_SEMS)
+UNIT_SEMS = 6
+CORE, X, Y, XY, YX, LAST = range(UNIT_SEMS)
 
 
 class Unit:
     def __init__(self, torus, refs, send_sem, recv_sem):
         self.t = torus
-        for (name, _, _), ref in zip(self.SCRATCH, refs):
+        for (name, _, _), ref in zip(STEP_SCRATCH, refs):
             setattr(self, name, ref)
         self.send_sem, self.recv_sem = send_sem, recv_sem
         self.sent = []
@@ -322,28 +321,47 @@
             wait_all(ref, self.send_sem.at[stage])
 
 
-class PlaneUnit(Unit):
-    SCRATCH = PLANE_SCRATCH
+    def _y_cols(self, dy=0):
+        return pl.ds(pl.multiple_of((self.t.y + dy) % 4 // 2 * 128, 128), 128)
 
     def spread(self):
         t = self.t
         self.core_total()
-        for dx, dy in PLANE:
-            y = (t.y + dy) % 4
-            cols = pl.ds(pl.multiple_of(y // 2 * 128, 128), 128)
-            slot = (-dx) % 4 * 4 + (-dy) % 4 - 1
+        for d in (2, 1, 3):
+            self._copy(self.half.at[0:4, (t.x + d) % 4], self.x_in.at[3 - d], X, t.in_plane(d, 0))
             self._copy(
-                self.half.at[:, (t.x + dx) % 4, y % 2, :, cols], self.plane_in.at[slot], MIDDLE, t.in_plane(dx, dy)
+                self.half.at[4:8, :, (t.y + d) % 2, :, self._y_cols(d)], self.y_in.at[3 - d], Y, t.in_plane(0, d)
             )
+
+    def turn(self):
+        t = self.t
+        self._arrived(X, self.x_in)
+        total = self.half[0:4, t.x].astype(F32)
+        for slot in range(3):
+            total = total + self.x_in[slot].astype(F32)
+        self.x_sum[...] = total.astype(BF16)
+        for d in (2, 1, 3):
+            self._copy(self.x_sum.at[:, (t.y + d) % 2, :, self._y_cols(d)], self.xy_in.at[3 - d], XY, t.in_plane(0, d))
+        self._arrived(Y, self.y_in)
+        total = self.half[4:8, :, t.y % 2, :, self._y_cols()].astype(F32)
+        for slot in range(3):
+            total = total + self.y_in[slot].astype(F32)
+        self.y_sum[...] = total.astype(BF16)
+        for d in (2, 1, 3):
+            self._copy(self.y_sum.at[:, (t.x + d) % 4], self.yx_in.at[3 - d], YX, t.in_plane(d, 0))
 
     def plane_total(self, sum_ref, place):
         t = self.t
-        self._arrived(MIDDLE, self.plane_in)
-        cols = pl.ds(pl.multiple_of(t.y // 2 * 128, 128), 128)
-        total = self.half[:, t.x, t.y % 2, :, cols].astype(F32)
-        for slot in range(15):
-            total = total + self.plane_in[slot].astype(F32)
-        sum_ref[:, place] = total.astype(BF16)
+        self._arrived(XY, self.xy_in)
+        total = self.x_sum[:, t.y % 2, :, self._y_cols()].astype(F32)
+        for slot in range(3):
+            total = total + self.xy_in[slot].astype(F32)
+        sum_ref[0:4, place] = total.astype(BF16)
+        self._arrived(YX, self.yx_in)
+        total = self.y_sum[:, t.x].astype(F32)
+        for slot in range(3):
+            total = total + self.yx_in[slot].astype(F32)
+        sum_ref[4:8, place] = total.astype(BF16)
 
 
 class Column:
@@ -381,42 +399,6 @@
 
     def close(self):
         wait_all(self.came, self.send_sem)
-
-
-class ZUnit(Unit):
-    SCRATCH = Z_SCRATCH
-
-    def spread(self):
-        t = self.t
-        self.core_total()
-        for dz in (4, 3, 5, 2, 6, 1, 7):
-            self._copy(self.half.at[(t.z + dz) % 8], self.z_in.at[7 - dz], MIDDLE, t.in_column(dz, 0))
-
-    def gather(self):
-        t = self.t
-        self._arrived(MIDDLE, self.z_in)
-        total = self.half[t.z].astype(F32)
-        for slot in range(7):
-            total = total + self.z_in[slot].astype(F32)
-        self.z_sum[...] = total.astype(BF16)
-        for dx, dy in PLANE:
-            slot = (-dx) % 4 * 4 + (-dy) % 4 - 1
-            self._copy(
-                self.z_sum.at[(t.x + dx) % 4, (t.y + dy) % 2], self.plane_in.at[slot], PLANE_LATE, t.in_plane(dx, dy)
-            )
-
-    def total(self):
-        t = self.t
-        self._arrived(PLANE_LATE, self.plane_in)
-        total = self.z_sum[t.x, t.y % 2].astype(F32)
-        for slot in range(15):
-            total = total + self.plane_in[slot].astype(F32)
-        self.last[t.core, 0] = total[:, 0:128]
-        self.last[t.core, 1] = total[:, 128:256]
-        self.send_last()
-
-
-UNIT_KINDS = (ZUnit, PlaneUnit, PlaneUnit, PlaneUnit)
 
 
 def kernel(
@@ -441,7 +423,7 @@
     n = len(BLOCK_SCRATCH)
     one, two = Block(scratch[:n]), Block(scratch[n : 2 * n])
     rest = list(scratch[2 * n :])
-    unit_refs = [[rest.pop(0) for _ in kind.SCRATCH] for kind in UNIT_KINDS]
+    unit_refs = [[rest.pop(0) for _ in STEP_SCRATCH] for _ in range(4)]
     (tokens_ref, cot_ref, land_ref, land_vec_ref, pole_vec_ref, w1_ref, o1_ref, w2_ref, o2_ref, cells_ref, mask_ref,
      sum2, sum1, came2, came1, halo_out, halo_in, load_sem, halo_send, halo_recv, red_send, red_recv, col_send,
      col_recv) = rest
@@ -490,9 +472,9 @@
         Halo(torus, i, sign, halo_out, halo_in, halo_send, halo_recv) for i, sign in enumerate((-1, -1, 1, 1))
     ]
     out2, query2, out1, query1 = (
-        kind(torus, refs, red_send.at[i], red_recv.at[i]) for i, (kind, refs) in enumerate(zip(UNIT_KINDS, unit_refs))
+        Unit(torus, refs, red_send.at[i], red_recv.at[i]) for i, refs in enumerate(unit_refs)
     )
-    column2 = Column(torus, [query2], sum2, came2, col_send.at[0], col_recv.at[0])
+    column2 = Column(torus, [query2, out2], sum2, came2, col_send.at[0], col_recv.at[0])
     column1 = Column(torus, [query1, out1], sum1, came1, col_send.at[1], col_recv.at[1])
 
     loads[4].wait()
@@ -532,28 +514,31 @@
 
     halos[3].receive(one.dy)
     backward_mixed(one, o1_ref)
+    backward_scores(one, range(HEADS))
+    query1.whole[...] = query_and_key_unit(one)
+    query1.start()
     backward_values(one)
     out1.whole[...] = output_and_value_unit(one)
     out1.start()
-    backward_scores(one, range(HEADS))
-    query1.whole[...] = query_and_key_unit(one)
-    query1.start()
+    query1.spread()
     out1.spread()
-    query1.spread()
 
     halos[2].receive(cells_ref)
     cells_to_field(cells_ref, layer_ref)
     cells_ref[...] = backward_input(one, w1_ref)
     cells_to_field(cells_ref, tokens_grad_ref)
-
+    out2.turn()
+    query2.turn()
+
+    query1.turn()
+    out1.turn()
+    out2.plane_total(sum2, 1)
     query2.plane_total(sum2, 0)
     column2.send()
-    out2.gather()
+    query1.plane_total(sum1, 0)
     out1.plane_total(sum1, 1)
-    query1.plane_total(sum1, 0)
     column1.send()
     column2.total()
-    out2.total()
     query2.finish(ga2_ref, 0, ga2_ref, D)
     out2.finish(go2_ref, 0, ga2_ref, 2 * D)
     column1.total()
@@ -597,7 +582,7 @@
         out_shape=shapes,
         in_specs=[hbm, hbm, smem, hbm, hbm, hbm, hbm, hbm, hbm, hbm],
         out_specs=[vmem] * 6,
-        scratch_shapes=[pltpu.VMEM(shape, dtype) for _, shape, dtype in BLOCK_SCRATCH * 2 + sum((k.SCRATCH for k in UNIT_KINDS), ())]
+        scratch_shapes=[pltpu.VMEM(shape, dtype) for _, shape, dtype in BLOCK_SCRATCH * 2 + STEP_SCRATCH * 4]
         + [
             pltpu.VMEM((WLAT, WLON, LV, D), BF16),
             pltpu.VMEM((WLAT, WLON, LV, D), BF16),
@@ -610,9 +595,9 @@
             pltpu.VMEM((D, D), BF16),
             pltpu.VMEM((CELLS, D), F32),
             pltpu.VMEM((CELLS, CELLS), F32),
-            pltpu.VMEM((NZ, 1, 16, 128), BF16),
             pltpu.VMEM((NZ, 2, 16, 128), BF16),
-            pltpu.VMEM((15, 1, 16, 128), BF16),
+            pltpu.VMEM((NZ, 2, 16, 128), BF16),
+            pltpu.VMEM((15, 2, 16, 128), BF16),
             pltpu.VMEM((15, 2, 16, 128), BF16),
             pltpu.VMEM((4, 3, SLAB, D), BF16),
             pltpu.VMEM((4, 3, SLAB, D), BF16),

time: 57 us -> 55.7 us (0.977)
  Pallas kernels: 55.8 us -> 54.9 us
    pallas_call x1, Pallas kernels: 54.1 us -> 53.2 us  [local(): pl.pallas_call(kernel, out_shape=shapes, in_specs=[hbm, hbm, smem, hbm, h...]
where the time goes in v4:
time: 55.7 us; the launch traced here: 55.6 us
  Pallas kernels  54.9 us (99%)
  between operations  0.64 us (1%)
    pallas_call x1, Pallas kernels, local(): pl.pallas_call(kernel, out_shape=shapes, in_specs=[hbm, hbm, smem, hbm, h...  53.2 us
    pallas_call x1, Pallas kernels, local(): pl.pallas_call(hand_over, out_shape=shapes, in_specs=[vmem] * 6, out_spec...  1.76 us

profile of v4, /device:TPU:1, one launch (start us, length us, event | category | flops | bytes accessed | tf_op | source)
XLA Modules:
  0.0 55.6 jit_solution(11869089020995002833)
XLA Ops:
  0.6 53.2 %shard_map.145 = (bf16[6,12,2,512]{3,2,1,0:T(2,128)(2,1)}, bf16[6,12,2,512]{3,2,1,0:T(2,128)(2,1)}, f32[8,1536]{1,0:T(8,128)}, f32[8,512]{1,0:T(8,128)}, f32[8,1536]{1,0:T(8,128)}, /*index=5*/f32[8,512]{1,0:T(8,128)}) custom-call(bf16[6,12,2,512]{3,2,1,0:T(2,128)(2,1)} %bitcast.4, s32[6,12]{1,0:T(8,128)} %land_hbm.1, s32[6]{0:T(128)} %pole_ref.1, ...), custom_call_target="tpu_custom_call" | custom-call | tf_op jit(solution)/shard_map/pallas_call | solution.py:580
  53.8 1.8 %shard_map.146 = (bf16[6,12,2,512]{3,2,1,0:T(2,128)(2,1)}, bf16[6,12,2,512]{3,2,1,0:T(2,128)(2,1)}, f32[8,1536]{1,0:T(8,128)}, f32[8,512]{1,0:T(8,128)}, f32[8,1536]{1,0:T(8,128)}, /*index=5*/f32[8,512]{1,0:T(8,128)}) custom-call(bf16[6,12,2,512]{3,2,1,0:T(2,128)(2,1)} %get-tuple-element.18.refs_0_, bf16[6,12,2,512]{3,2,1,0:T(2,128)(2,1)} %get-tuple-element.19.refs_1_, ...), custom_call_target="tpu_custom_call" | custom-call | tf_op jit(solution)/shard_map/pallas_call | solution.py:627

commit v5 on v4

--- a/solution.py
+++ b/solution.py
@@ -254,28 +254,30 @@
         wait_all(self.out_ref, self.send_sem)
 
 
-UNIT_SCRATCH = (
-    ("whole", (NZ, NX, NYL, 16, D), BF16),
-    ("core_in", (NZ, NX, NYL, 16, 256), BF16),
-    ("half", (NZ, NX, NYL, 16, 256), BF16),
-    ("last", (2, 2, 16, 128), F32),
-)
-STEP_SCRATCH = UNIT_SCRATCH + (
-    ("x_in", (3, 4, NYL, 16, 256), BF16),
-    ("x_sum", (4, NYL, 16, 256), BF16),
-    ("y_in", (3, 4, NX, 16, 128), BF16),
-    ("y_sum", (4, NX, 16, 128), BF16),
-    ("xy_in", (3, 4, 16, 128), BF16),
-    ("yx_in", (3, 4, 16, 128), BF16),
-)
+def group_scratch(n):
+    return (
+        ("whole", (n, NZ, NX, NYL, 16, D), BF16),
+        ("core_in", (n, NZ, NX, NYL, 16, 256), BF16),
+        ("half", (n, NZ, NX, NYL, 16, 256), BF16),
+        ("x_in", (3, n, 4, NYL, 16, 256), BF16),
+        ("x_sum", (n, 4, NYL, 16, 256), BF16),
+        ("y_in", (3, n, 4, NX, 16, 128), BF16),
+        ("y_sum", (n, 4, NX, 16, 128), BF16),
+        ("xy_in", (3, n, 4, 16, 128), BF16),
+        ("yx_in", (3, n, 4, 16, 128), BF16),
+        ("last", (2, 2, n, 16, 128), F32),
+    )
+
+
+GROUPS = (2, 2)
 UNIT_SEMS = 6
 CORE, X, Y, XY, YX, LAST = range(UNIT_SEMS)
 
 
-class Unit:
-    def __init__(self, torus, refs, send_sem, recv_sem):
-        self.t = torus
-        for (name, _, _), ref in zip(STEP_SCRATCH, refs):
+class Group:
+    def __init__(self, torus, n, refs, send_sem, recv_sem):
+        self.t, self.n = torus, n
+        for (name, _, _), ref in zip(group_scratch(n), refs):
             setattr(self, name, ref)
         self.send_sem, self.recv_sem = send_sem, recv_sem
         self.sent = []
@@ -294,32 +296,33 @@
         wait_all(ref, self.recv_sem.at[stage])
         self.sent.append((stage, ref))
 
-    def start(self):
+    def start(self, unit, gradients):
         t = self.t
+        self.whole[unit] = gradients
         cols = pl.ds(pl.multiple_of((1 - t.core) * 256, 256), 256)
-        self._copy(self.whole.at[:, :, :, :, cols], self.core_in, CORE, t.at(core=1 - t.core))
+        self._copy(self.whole.at[unit, :, :, :, :, cols], self.core_in.at[unit], CORE, t.at(core=1 - t.core))
 
     def core_total(self):
         self._arrived(CORE, self.core_in)
         cols = pl.ds(pl.multiple_of(self.t.core * 256, 256), 256)
-        self.half[...] = (self.whole[:, :, :, :, cols].astype(F32) + self.core_in[...].astype(F32)).astype(BF16)
+        self.half[...] = self.whole[:, :, :, :, :, cols] + self.core_in[...]
 
     def send_last(self):
         t = self.t
         self._copy(self.last.at[t.core], self.last.at[t.core], LAST, t.at(core=1 - t.core))
 
-    def finish(self, first_ref, first_col, second_ref, second_col):
-        self._arrived(LAST, self.last.at[1 - self.t.core])
+    def finish(self, unit, first_ref, first_col, second_ref, second_col):
+        if unit == 0:
+            self._arrived(LAST, self.last.at[1 - self.t.core])
         for core in range(2):
             for high in range(2):
                 off = core * 256 + high * 128
-                first_ref[:, first_col + off : first_col + off + 128] = self.last[core, high, 0:8, :]
-                second_ref[:, second_col + off : second_col + off + 128] = self.last[core, high, 8:16, :]
+                first_ref[:, first_col + off : first_col + off + 128] = self.last[core, high, unit, 0:8, :]
+                second_ref[:, second_col + off : second_col + off + 128] = self.last[core, high, unit, 8:16, :]
 
     def close(self):
         for stage, ref in self.sent:
             wait_all(ref, self.send_sem.at[stage])
-
 
     def _y_cols(self, dy=0):
         return pl.ds(pl.multiple_of((self.t.y + dy) % 4 // 2 * 128, 128), 128)
@@ -328,45 +331,49 @@
         t = self.t
         self.core_total()
         for d in (2, 1, 3):
-            self._copy(self.half.at[0:4, (t.x + d) % 4], self.x_in.at[3 - d], X, t.in_plane(d, 0))
+            self._copy(self.half.at[:, 0:4, (t.x + d) % 4], self.x_in.at[3 - d], X, t.in_plane(d, 0))
             self._copy(
-                self.half.at[4:8, :, (t.y + d) % 2, :, self._y_cols(d)], self.y_in.at[3 - d], Y, t.in_plane(0, d)
+                self.half.at[:, 4:8, :, (t.y + d) % 2, :, self._y_cols(d)], self.y_in.at[3 - d], Y, t.in_plane(0, d)
             )
 
     def turn(self):
         t = self.t
         self._arrived(X, self.x_in)
-        total = self.half[0:4, t.x].astype(F32)
+        total = self.half[:, 0:4, t.x].astype(F32)
         for slot in range(3):
             total = total + self.x_in[slot].astype(F32)
         self.x_sum[...] = total.astype(BF16)
         for d in (2, 1, 3):
-            self._copy(self.x_sum.at[:, (t.y + d) % 2, :, self._y_cols(d)], self.xy_in.at[3 - d], XY, t.in_plane(0, d))
+            self._copy(
+                self.x_sum.at[:, :, (t.y + d) % 2, :, self._y_cols(d)], self.xy_in.at[3 - d], XY, t.in_plane(0, d)
+            )
         self._arrived(Y, self.y_in)
-        total = self.half[4:8, :, t.y % 2, :, self._y_cols()].astype(F32)
+        total = self.half[:, 4:8, :, t.y % 2, :, self._y_cols()].astype(F32)
         for slot in range(3):
             total = total + self.y_in[slot].astype(F32)
         self.y_sum[...] = total.astype(BF16)
         for d in (2, 1, 3):
-            self._copy(self.y_sum.at[:, (t.x + d) % 4], self.yx_in.at[3 - d], YX, t.in_plane(d, 0))
+            self._copy(self.y_sum.at[:, :, (t.x + d) % 4], self.yx_in.at[3 - d], YX, t.in_plane(d, 0))
 
     def plane_total(self, sum_ref, place):
         t = self.t
         self._arrived(XY, self.xy_in)
-        total = self.x_sum[:, t.y % 2, :, self._y_cols()].astype(F32)
+        total = self.x_sum[:, :, t.y % 2, :, self._y_cols()].astype(F32)
         for slot in range(3):
             total = total + self.xy_in[slot].astype(F32)
-        sum_ref[0:4, place] = total.astype(BF16)
+        for unit in range(self.n):
+            sum_ref[0:4, place + unit] = total[unit].astype(BF16)
         self._arrived(YX, self.yx_in)
-        total = self.y_sum[:, t.x].astype(F32)
+        total = self.y_sum[:, :, t.x].astype(F32)
         for slot in range(3):
             total = total + self.yx_in[slot].astype(F32)
-        sum_ref[4:8, place] = total.astype(BF16)
+        for unit in range(self.n):
+            sum_ref[4:8, place + unit] = total[unit].astype(BF16)
 
 
 class Column:
-    def __init__(self, torus, units, sum_ref, in_ref, send_sem, recv_sem):
-        self.t, self.units, self.sum, self.came = torus, units, sum_ref, in_ref
+    def __init__(self, torus, groups, sum_ref, in_ref, send_sem, recv_sem):
+        self.t, self.groups, self.sum, self.came = torus, groups, sum_ref, in_ref
         self.send_sem, self.recv_sem = send_sem, recv_sem
 
     def send(self):
@@ -392,10 +399,12 @@
         for dz in range(1, 8):
             other = other + self.came[dz * 2].astype(F32)
         high = t.y // 2
-        for place, unit in enumerate(self.units):
-            unit.last[t.core, high] = mine[place]
-            unit.last[t.core, 1 - high] = other[place]
-            unit.send_last()
+        place = 0
+        for group in self.groups:
+            group.last[t.core, high] = mine[place : place + group.n]
+            group.last[t.core, 1 - high] = other[place : place + group.n]
+            group.send_last()
+            place += group.n
 
     def close(self):
         wait_all(self.came, self.send_sem)
@@ -423,7 +432,7 @@
     n = len(BLOCK_SCRATCH)
     one, two = Block(scratch[:n]), Block(scratch[n : 2 * n])
     rest = list(scratch[2 * n :])
-    unit_refs = [[rest.pop(0) for _ in STEP_SCRATCH] for _ in range(4)]
+    unit_refs = [[rest.pop(0) for _ in group_scratch(n)] for n in GROUPS]
     (tokens_ref, cot_ref, land_ref, land_vec_ref, pole_vec_ref, w1_ref, o1_ref, w2_ref, o2_ref, cells_ref, mask_ref,
      sum2, sum1, came2, came1, halo_out, halo_in, load_sem, halo_send, halo_recv, red_send, red_recv, col_send,
      col_recv) = rest
@@ -471,11 +480,11 @@
     halos = [
         Halo(torus, i, sign, halo_out, halo_in, halo_send, halo_recv) for i, sign in enumerate((-1, -1, 1, 1))
     ]
-    out2, query2, out1, query1 = (
-        Unit(torus, refs, red_send.at[i], red_recv.at[i]) for i, refs in enumerate(unit_refs)
+    both2, both1 = (
+        Group(torus, n, refs, red_send.at[i], red_recv.at[i]) for i, (n, refs) in enumerate(zip(GROUPS, unit_refs))
     )
-    column2 = Column(torus, [query2, out2], sum2, came2, col_send.at[0], col_recv.at[0])
-    column1 = Column(torus, [query1, out1], sum1, came1, col_send.at[1], col_recv.at[1])
+    column2 = Column(torus, [both2], sum2, came2, col_send.at[0], col_recv.at[0])
+    column1 = Column(torus, [both1], sum1, came1, col_send.at[1], col_recv.at[1])
 
     loads[4].wait()
     loads[5].wait()
@@ -505,46 +514,36 @@
     backward_scores(two, range(HEADS))
     one.dy[...] = backward_input(two, w2_ref)
     halos[3].send(one.dy)
-    out2.whole[...] = output_and_value_unit(two)
-    out2.start()
-    query2.whole[...] = query_and_key_unit(two)
-    query2.start()
-    out2.spread()
-    query2.spread()
+    both2.start(0, output_and_value_unit(two))
+    both2.start(1, query_and_key_unit(two))
+    both2.spread()
 
     halos[3].receive(one.dy)
     backward_mixed(one, o1_ref)
     backward_scores(one, range(HEADS))
-    query1.whole[...] = query_and_key_unit(one)
-    query1.start()
+    both1.start(0, query_and_key_unit(one))
     backward_values(one)
-    out1.whole[...] = output_and_value_unit(one)
-    out1.start()
-    query1.spread()
-    out1.spread()
+    both1.start(1, output_and_value_unit(one))
+    both1.spread()
 
     halos[2].receive(cells_ref)
     cells_to_field(cells_ref, layer_ref)
     cells_ref[...] = backward_input(one, w1_ref)
     cells_to_field(cells_ref, tokens_grad_ref)
-    out2.turn()
-    query2.turn()
-
-    query1.turn()
-    out1.turn()
-    out2.plane_total(sum2, 1)
-    query2.plane_total(sum2, 0)
+    both2.turn()
+
+    both1.turn()
+    both2.plane_total(sum2, 0)
     column2.send()
-    query1.plane_total(sum1, 0)
-    out1.plane_total(sum1, 1)
+    both1.plane_total(sum1, 0)
     column1.send()
     column2.total()
-    query2.finish(ga2_ref, 0, ga2_ref, D)
-    out2.finish(go2_ref, 0, ga2_ref, 2 * D)
+    both2.finish(0, go2_ref, 0, ga2_ref, 2 * D)
+    both2.finish(1, ga2_ref, 0, ga2_ref, D)
     column1.total()
-    query1.finish(ga1_ref, 0, ga1_ref, D)
-    out1.finish(go1_ref, 0, ga1_ref, 2 * D)
-    for each in halos + [out2, query2, out1, query1, column2, column1]:
+    both1.finish(0, ga1_ref, 0, ga1_ref, D)
+    both1.finish(1, go1_ref, 0, ga1_ref, 2 * D)
+    for each in halos + [both2, both1, column2, column1]:
         each.close()
 
 
@@ -582,7 +581,7 @@
         out_shape=shapes,
         in_specs=[hbm, hbm, smem, hbm, hbm, hbm, hbm, hbm, hbm, hbm],
         out_specs=[vmem] * 6,
-        scratch_shapes=[pltpu.VMEM(shape, dtype) for _, shape, dtype in BLOCK_SCRATCH * 2 + STEP_SCRATCH * 4]
+        scratch_shapes=[pltpu.VMEM(shape, dtype) for _, shape, dtype in BLOCK_SCRATCH * 2 + sum((group_scratch(n) for n in GROUPS), ())]
         + [
             pltpu.VMEM((WLAT, WLON, LV, D), BF16),
             pltpu.VMEM((WLAT, WLON, LV, D), BF16),
@@ -604,8 +603,8 @@
             pltpu.SemaphoreType.DMA((9,)),
             pltpu.SemaphoreType.DMA((4,)),
             pltpu.SemaphoreType.DMA((4,)),
-            pltpu.SemaphoreType.DMA((4, UNIT_SEMS)),
-            pltpu.SemaphoreType.DMA((4, UNIT_SEMS)),
+            pltpu.SemaphoreType.DMA((2, UNIT_SEMS)),
+            pltpu.SemaphoreType.DMA((2, UNIT_SEMS)),
             pltpu.SemaphoreType.DMA((2,)),
             pltpu.SemaphoreType.DMA((2,)),
         ],

time: 55.7 us -> 54.6 us (0.980)
  Pallas kernels: 54.9 us -> 53.8 us
    pallas_call x1, Pallas kernels: 53.2 us -> 52.1 us  [local(): pl.pallas_call(kernel, out_shape=shapes, in_specs=[hbm, hbm, smem, hbm, h...]
where the time goes in v5:
time: 54.6 us; the launch traced here: 54.5 us
  Pallas kernels  53.8 us (99%)
  between operations  0.64 us (1%)
    pallas_call x1, Pallas kernels, local(): pl.pallas_call(kernel, out_shape=shapes, in_specs=[hbm, hbm, smem, hbm, h...  52.1 us
    pallas_call x1, Pallas kernels, local(): pl.pallas_call(hand_over, out_shape=shapes, in_specs=[vmem] * 6, out_spec...  1.76 us

profile of v5, /device:TPU:1, one launch (start us, length us, event | category | flops | bytes accessed | tf_op | source)
XLA Modules:
  0.0 54.5 jit_solution(6880151500229276349)
XLA Ops:
  0.6 52.1 %shard_map.145 = (bf16[6,12,2,512]{3,2,1,0:T(2,128)(2,1)}, bf16[6,12,2,512]{3,2,1,0:T(2,128)(2,1)}, f32[8,1536]{1,0:T(8,128)}, f32[8,512]{1,0:T(8,128)}, f32[8,1536]{1,0:T(8,128)}, /*index=5*/f32[8,512]{1,0:T(8,128)}) custom-call(bf16[6,12,2,512]{3,2,1,0:T(2,128)(2,1)} %bitcast.4, s32[6,12]{1,0:T(8,128)} %land_hbm.1, s32[6]{0:T(128)} %pole_ref.1, ...), custom_call_target="tpu_custom_call" | custom-call | tf_op jit(solution)/shard_map/pallas_call | solution.py:579
  52.7 1.8 %shard_map.146 = (bf16[6,12,2,512]{3,2,1,0:T(2,128)(2,1)}, bf16[6,12,2,512]{3,2,1,0:T(2,128)(2,1)}, f32[8,1536]{1,0:T(8,128)}, f32[8,512]{1,0:T(8,128)}, f32[8,1536]{1,0:T(8,128)}, /*index=5*/f32[8,512]{1,0:T(8,128)}) custom-call(bf16[6,12,2,512]{3,2,1,0:T(2,128)(2,1)} %get-tuple-element.18.refs_0_, bf16[6,12,2,512]{3,2,1,0:T(2,128)(2,1)} %get-tuple-element.19.refs_1_, ...), custom_call_target="tpu_custom_call" | custom-call | tf_op jit(solution)/shard_map/pallas_call | solution.py:626

commit v6 on v5

--- a/solution.py
+++ b/solution.py
@@ -506,7 +506,6 @@
     loads[8].wait()
     halos[0].receive(two.u)
     cells_ref[...] = forward(two, w2_ref, o2_ref, mask_ref)
-    halos[2].send(cells_ref)
     halos[1].receive(two.dy)
 
     backward_mixed(two, o2_ref)
@@ -524,15 +523,16 @@
     both1.start(0, query_and_key_unit(one))
     backward_values(one)
     both1.start(1, output_and_value_unit(one))
+    halos[2].send(cells_ref)
     both1.spread()
 
+    two.u[...] = backward_input(one, w1_ref)
+    cells_to_field(two.u, tokens_grad_ref)
+    both2.turn()
+
+    both1.turn()
     halos[2].receive(cells_ref)
     cells_to_field(cells_ref, layer_ref)
-    cells_ref[...] = backward_input(one, w1_ref)
-    cells_to_field(cells_ref, tokens_grad_ref)
-    both2.turn()
-
-    both1.turn()
     both2.plane_total(sum2, 0)
     column2.send()
     both1.plane_total(sum1, 0)

time: 54.6 us -> 56.4 us (1.033)
  Pallas kernels: 53.8 us -> 55.6 us
    pallas_call x1, Pallas kernels: 52.1 us -> 53.8 us  [local(): pl.pallas_call(kernel, out_shape=shapes, in_specs=[hbm, hbm, smem, hbm, h...]
where the time goes in v6:
time: 56.4 us; the launch traced here: 56.2 us
  Pallas kernels  55.6 us (99%)
  between operations  0.64 us (1%)
    pallas_call x1, Pallas kernels, local(): pl.pallas_call(kernel, out_shape=shapes, in_specs=[hbm, hbm, smem, hbm, h...  53.8 us
    pallas_call x1, Pallas kernels, local(): pl.pallas_call(hand_over, out_shape=shapes, in_specs=[vmem] * 6, out_spec...  1.76 us

profile of v6, /device:TPU:1, one launch (start us, length us, event | category | flops | bytes accessed | tf_op | source)
XLA Modules:
  0.0 56.2 jit_solution(16427660292549827849)
XLA Ops:
  0.6 53.8 %shard_map.145 = (bf16[6,12,2,512]{3,2,1,0:T(2,128)(2,1)}, bf16[6,12,2,512]{3,2,1,0:T(2,128)(2,1)}, f32[8,1536]{1,0:T(8,128)}, f32[8,512]{1,0:T(8,128)}, f32[8,1536]{1,0:T(8,128)}, /*index=5*/f32[8,512]{1,0:T(8,128)}) custom-call(bf16[6,12,2,512]{3,2,1,0:T(2,128)(2,1)} %bitcast.4, s32[6,12]{1,0:T(8,128)} %land_hbm.1, s32[6]{0:T(128)} %pole_ref.1, ...), custom_call_target="tpu_custom_call" | custom-call | tf_op jit(solution)/shard_map/pallas_call | solution.py:579
  54.5 1.8 %shard_map.146 = (bf16[6,12,2,512]{3,2,1,0:T(2,128)(2,1)}, bf16[6,12,2,512]{3,2,1,0:T(2,128)(2,1)}, f32[8,1536]{1,0:T(8,128)}, f32[8,512]{1,0:T(8,128)}, f32[8,1536]{1,0:T(8,128)}, /*index=5*/f32[8,512]{1,0:T(8,128)}) custom-call(bf16[6,12,2,512]{3,2,1,0:T(2,128)(2,1)} %get-tuple-element.18.refs_0_, bf16[6,12,2,512]{3,2,1,0:T(2,128)(2,1)} %get-tuple-element.19.refs_1_, ...), custom_call_target="tpu_custom_call" | custom-call | tf_op jit(solution)/shard_map/pallas_call | solution.py:626
